TPU v7x, 32 devices: a whole 2x2x4 slice. The times are simulated.
32 devices in a mesh: outer: 4 (over z), inner: 8 (over y, x, core).
Axes of the slice: x: 2, y: 2, z: 4, core: 2. Of those that a mesh axis runs over, the one named last changes fastest.
Arguments:
- query_rot: bfloat16 [4, 1024, 896], P('outer', 'inner'), may hold values from -6 to 6
- key_rot: bfloat16 [4, 1024, 128], P('outer', 'inner'), may hold values from -6 to 6
- value_rows: bfloat16 [4, 1024, 128], P('outer', 'inner'), may hold values from -6 to 6
- attention_out: bfloat16 [4, 1024, 896], P('outer', 'inner'), may hold values from -6 to 6
- grad_out: bfloat16 [4, 1024, 896], P('outer', 'inner'), may hold values from -12 to 12
- log_norm: float32 [4, 7, 1024], P('outer', None, 'inner'), may hold values from 7.5 to 9
- segments: int32 [1, 1024], P(None, 'inner'), may hold values from 0 to 2, as said below
- block_table: int32 [1, 8, 8], P(None, 'inner'), may hold values from 0 to 1, as said below
Outputs:
- grad_query: bfloat16 [4, 1024, 896], P('outer', 'inner')
- grad_key: bfloat16 [4, 1024, 128], P('outer', 'inner')
- grad_value: bfloat16 [4, 1024, 128], P('outer', 'inner')
- grad_bias: float32 [4608], replicated
Inputs may be any that keep to these rules, and one draw needn't show every extreme that they name: `segments`: in every example the tokens of segment 0 come first, then those of segment 1, then those of segment 2; each segment is present. block_table[e,a,b] is 1 exactly when some token of block a (tokens a * 128 to a * 128 + 127) and some token of block b of example e have segments s_q and s_k with s_k == 0 or s_k == s_q, else 0.
All inputs are finite; a program needn't handle non-finite values.
Results may differ from a plain program's by a relative error of at most 0.0056.
Values may be sent and summed in bfloat16 or wider, within the bound.
A program may use at most 64 MiB of HBM per device.

v0:
```python
import math

import jax
import jax.numpy as jnp
from jax import lax
from jax.sharding import PartitionSpec as P

HEADS = 28
KV_HEADS = 4
HEAD_DIM = 128
BIAS = 4608


ROPE_BASE = 1000000.0


def passed_along(value, axis, steps):
    count = lax.axis_size(axis)
    pairs = [(source, (source + steps) % count) for source in range(count)]
    return lax.ppermute(value, axis, pairs)


def unrotate(gradient, positions, heads):
    rows_here = gradient.shape[0]
    halfway = HEAD_DIM // 2
    per_head = gradient.reshape(rows_here, heads, HEAD_DIM)
    frequency = jnp.exp(
        jnp.arange(halfway, dtype=jnp.float32) * (-2.0 * math.log(ROPE_BASE) / HEAD_DIM)
    )
    angles = positions[:, None] * frequency[None, :]
    cosine = jnp.cos(angles)[:, None, :]
    sine_term = jnp.sin(angles)[:, None, :]
    first_half = per_head[..., :halfway]
    second_half = per_head[..., halfway:]
    joined = jnp.concatenate(
        [
            first_half * cosine + second_half * sine_term,
            second_half * cosine - first_half * sine_term,
        ],
        axis=-1,
    )
    return joined.reshape(rows_here, heads * HEAD_DIM)


def local(query_rot, key_rot, value_rows, attention_out, grad_out, log_norm, segments, block_table):
    rows_here = query_rot.shape[1]
    group_size = HEADS // KV_HEADS
    scaling = HEAD_DIM ** (-0.5)
    members = lax.axis_size("inner")
    my_index = lax.axis_index("inner")
    outer_index = lax.axis_index("outer")
    example = outer_index // KV_HEADS
    head_index = outer_index % KV_HEADS
    queries = query_rot[0].reshape(rows_here, group_size, HEAD_DIM)
    grads_out = grad_out[0].reshape(rows_here, group_size, HEAD_DIM)
    products = grad_out[0].astype(jnp.float32) * attention_out[0].astype(jnp.float32)
    deltas = jnp.transpose(
        jnp.sum(products.reshape(rows_here, group_size, HEAD_DIM), axis=-1), (1, 0)
    )
    norms = log_norm[0]
    seg_query = lax.dynamic_index_in_dim(segments, example, 0, keepdims=False)
    seg_every = lax.all_gather(segments, "inner", axis=1, tiled=True)
    seg_all = lax.dynamic_index_in_dim(seg_every, example, 0, keepdims=False)
    table_row = lax.dynamic_index_in_dim(block_table[:, 0, :], example, 0, keepdims=False)
    own_pair = (key_rot[0], value_rows[0])
    query_zero = jnp.zeros((rows_here, group_size, HEAD_DIM), jnp.float32)
    kv_zero = jnp.zeros((rows_here, HEAD_DIM), jnp.float32)

    def contribution(pair, source):
        keys_here = pair[0]
        values_here = pair[1]
        seg_key = lax.dynamic_slice_in_dim(seg_all, source * rows_here, rows_here, 0)

        def compute(unused):
            allowed = (seg_key[None, :] == 0) | (seg_key[None, :] == seg_query[:, None])
            scores = (
                jnp.einsum("tgd,ud->gtu", queries, keys_here, preferred_element_type=jnp.float32)
                * scaling
            )
            probs = jnp.where(allowed[None], jnp.exp(scores - norms[..., None]), 0.0)
            probs_low = probs.astype(jnp.bfloat16)
            grad_probs = jnp.einsum(
                "tgd,ud->gtu", grads_out, values_here, preferred_element_type=jnp.float32
            )
            scores_low = (probs * (grad_probs - deltas[..., None])).astype(jnp.bfloat16)
            value_part = jnp.einsum(
                "gtu,tgd->ud", probs_low, grads_out, preferred_element_type=jnp.float32
            )
            key_part = jnp.einsum(
                "gtu,tgd->ud", scores_low, queries, preferred_element_type=jnp.float32
            )
            query_part = jnp.einsum(
                "gtu,ud->tgd", scores_low, keys_here, preferred_element_type=jnp.float32
            )
            return (query_part, key_part, value_part)

        def nothing(unused):
            return (query_zero, kv_zero, kv_zero)

        return lax.cond(table_row[source] > 0, compute, nothing, 0)

    own_query, own_key, own_value = contribution(own_pair, my_index)

    def pass_blocks(pair):
        return passed_along((pair[0], pair[1]), "inner", 1)

    def pass_grads(grads):
        return passed_along((grads[0], grads[1]), "inner", 1)

    def one_turn(step_index, carry):
        pair, grads, query_acc = carry
        pair = pass_blocks(pair)
        grads = pass_grads(grads)
        query_part, key_part, value_part = contribution(pair, (my_index - step_index) % members)
        return (pair, (grads[0] + key_part, grads[1] + value_part), query_acc + query_part)

    last_pair, grads, query_acc = lax.fori_loop(
        1, members, one_turn, (own_pair, (own_key, own_value), own_query)
    )
    home = pass_grads(grads)
    key_sum = home[0]
    value_sum = home[1]
    positions = (my_index * rows_here + jnp.arange(rows_here, dtype=jnp.int32)).astype(jnp.float32)
    query_full = unrotate(
        query_acc.reshape(rows_here, group_size * HEAD_DIM) * scaling, positions, group_size
    )
    key_full = unrotate(key_sum * scaling, positions, 1)
    bias_local = jnp.zeros((BIAS,), jnp.float32)
    bias_local = lax.dynamic_update_slice_in_dim(
        bias_local, jnp.sum(query_full, axis=0), head_index * (group_size * HEAD_DIM), 0
    )
    bias_local = lax.dynamic_update_slice_in_dim(
        bias_local, jnp.sum(key_full, axis=0), HEADS * HEAD_DIM + head_index * HEAD_DIM, 0
    )
    bias_local = lax.dynamic_update_slice_in_dim(
        bias_local,
        jnp.sum(value_sum, axis=0),
        HEADS * HEAD_DIM + KV_HEADS * HEAD_DIM + head_index * HEAD_DIM,
        0,
    )
    grad_bias = lax.psum(bias_local, ("outer", "inner"))
    return (
        query_full.astype(jnp.bfloat16)[None],
        key_full.astype(jnp.bfloat16)[None],
        value_sum.astype(jnp.bfloat16)[None],
        grad_bias,
    )


def solution(mesh):
    placed = (
        P("outer", "inner", None),
        P("outer", "inner", None),
        P("outer", "inner", None),
        P("outer", "inner", None),
        P("outer", "inner", None),
        P("outer", None, "inner"),
        P(None, "inner"),
        P(None, "inner", None),
    )
    return jax.shard_map(
        local,
        mesh=mesh,
        in_specs=placed,
        out_specs=(
            P("outer", "inner", None),
            P("outer", "inner", None),
            P("outer", "inner", None),
            P(),
        ),
        check_vma=False,
    )
```

profile of v0, /device:TPU:0, one launch (start us, length us, event | category | flops | bytes accessed | tf_op | source)
XLA Modules:
  0.0 118.5 jit_solution(9385778188579293595)
XLA Ops:
  0.6 0.8 copy.71
  1.4 1.1 copy.20
  3.0 0.9 copy-done.1
  4.1 0.5 copy-done.3
  4.5 10.2 %all_gather.3 = s32[1,1024]{1,0:T(1,128)S(1)} all-gather(s32[1,128]{1,0:T(1,128)S(1)} %copy-done.3), channel_id=1, replica_groups=mesh['outer'=4,'inner'=8] {'inner'}, dimensions={1}, use_global_device_ids=true | all-gather | bytes 4608 | tf_op jit(solution)/shard_map/all_gather | solution.py:62
  14.7 0.7 copy-done.5
  15.4 0.6 fusion.33
  16.8 0.5 copy-done.4
  17.3 1.4 %conditional.2 = (f32[128,7,128]{2,0,1:T(8,128)S(1)}, f32[128,128]{1,0:T(8,128)S(1)}, f32[128,128]{1,0:T(8,128)S(1)}) conditional(s32[]{:T(128)} %bitcast.20, () %tuple.58, (s32[]{:T(128)}, s32[1,1024]{1,0:T(1,128)S(1)}, s32[128]{0:T(128)S(1)}, bf16[128,128]{1,0:T(8,128)(2,1)S(1)}, bf16[128,7,128]{0,2,1:T(8,128)(2,1)S(1)}, ...), branch_computations={%region_1.2_spmd, %region_2.3_spmd} | conditional | flops 147636352 | bytes 3719486 | solution.py:100
  18.0 0.3 convolution_bitcast_fusion
  18.7 53.0 %while.23 = (s32[]{:T(128)}, bf16[128,128]{1,0:T(8,128)(2,1)S(1)}, bf16[128,128]{1,0:T(8,128)(2,1)S(1)}, f32[128,128]{1,0:T(8,128)S(1)}, f32[128,128]{1,0:T(8,12...) while((s32[]{:T(128)}, bf16[128,128]{1,0:T(8,128)(2,1)S(1)}, ...), condition=%wide.region_6.7_spmd, body=%wide.region_3.6_spmd.sunk | while | flops 147783824 | bytes 6399892 | solution.py:117
  18.7 0.4 collective-permute-start.3
  19.1 1.3 %collective-permute-start.2 = (f32[128,128]{1,0:T(8,128)S(1)}, f32[128,128]{1,0:T(8,128)S(1)}, u32[]{:S(2)}, u32[]{:S(2)}) collective-permute-start(f32[128,128]{1,0:T(8,128)S(1)} %get-tuple-element.707), channel_id=1, source_target_pairs={{0,1},{1,2},{2,3},{3,4},{4,5},{5,6},{6,7},{7,0},{8,9},{9,10},{10,1... | collective-permute-start | bytes 196616 | tf_op jit(solution)/shard_map/while/body/eval_jaxpr/ppermute | solution.py:20
  20.4 0.3 collective-permute-start
  20.7 1.2 %collective-permute-start.1 = (bf16[128,128]{1,0:T(8,128)(2,1)S(1)}, bf16[128,128]{1,0:T(8,128)(2,1)S(1)}, u32[]{:S(2)}, u32[]{:S(2)}) collective-permute-start(bf16[128,128]{1,0:T(8,128)(2,1)S(1)} %get-tuple-element.706), channel_id=1, source_target_pairs={{0,1},{1,2},{2,3},{3,4},{4,5},{5,6},{6,7},{7,0},{8,9},{9,10},{10,1... | collective-permute-start | bytes 98312 | tf_op jit(solution)/shard_map/while/body/eval_jaxpr/ppermute | solution.py:20
  22.0 0.6 dynamic_slice.41
  23.2 1.4 %collective-permute-done = bf16[128,128]{1,0:T(8,128)(2,1)S(1)} collective-permute-done((bf16[128,128]{1,0:T(8,128)(2,1)S(1)}, bf16[128,128]{1,0:T(8,128)(2,1)S(1)}, u32[]{:S(2)}, u32[]{:S(2)}) %collective-permute-start) | collective-permute-done | bytes 32800 | tf_op jit(solution)/shard_map/while/body/eval_jaxpr/ppermute | solution.py:20
  24.6 0.4 collective-permute-done.1
  25.3 2.0 %collective-permute-start.2 = (f32[128,128]{1,0:T(8,128)S(1)}, f32[128,128]{1,0:T(8,128)S(1)}, u32[]{:S(2)}, u32[]{:S(2)}) collective-permute-start(f32[128,128]{1,0:T(8,128)S(1)} %get-tuple-element.707), channel_id=1, source_target_pairs={{0,1},{1,2},{2,3},{3,4},{4,5},{5,6},{6,7},{7,0},{8,9},{9,10},{10,1... | collective-permute-start | bytes 196616 | tf_op jit(solution)/shard_map/while/body/eval_jaxpr/ppermute | solution.py:20
  27.4 2.2 %collective-permute-start.1 = (bf16[128,128]{1,0:T(8,128)(2,1)S(1)}, bf16[128,128]{1,0:T(8,128)(2,1)S(1)}, u32[]{:S(2)}, u32[]{:S(2)}) collective-permute-start(bf16[128,128]{1,0:T(8,128)(2,1)S(1)} %get-tuple-element.706), channel_id=1, source_target_pairs={{0,1},{1,2},{2,3},{3,4},{4,5},{5,6},{6,7},{7,0},{8,9},{9,10},{10,1... | collective-permute-start | bytes 98312 | tf_op jit(solution)/shard_map/while/body/eval_jaxpr/ppermute | solution.py:20
  29.6 0.6 dynamic_slice.41
  30.8 0.7 collective-permute-done
  31.5 0.4 collective-permute-done.1
  32.2 2.7 %collective-permute-start.2 = (f32[128,128]{1,0:T(8,128)S(1)}, f32[128,128]{1,0:T(8,128)S(1)}, u32[]{:S(2)}, u32[]{:S(2)}) collective-permute-start(f32[128,128]{1,0:T(8,128)S(1)} %get-tuple-element.707), channel_id=1, source_target_pairs={{0,1},{1,2},{2,3},{3,4},{4,5},{5,6},{6,7},{7,0},{8,9},{9,10},{10,1... | collective-permute-start | bytes 196616 | tf_op jit(solution)/shard_map/while/body/eval_jaxpr/ppermute | solution.py:20
  35.0 2.2 %collective-permute-start.1 = (bf16[128,128]{1,0:T(8,128)(2,1)S(1)}, bf16[128,128]{1,0:T(8,128)(2,1)S(1)}, u32[]{:S(2)}, u32[]{:S(2)}) collective-permute-start(bf16[128,128]{1,0:T(8,128)(2,1)S(1)} %get-tuple-element.706), channel_id=1, source_target_pairs={{0,1},{1,2},{2,3},{3,4},{4,5},{5,6},{6,7},{7,0},{8,9},{9,10},{10,1... | collective-permute-start | bytes 98312 | tf_op jit(solution)/shard_map/while/body/eval_jaxpr/ppermute | solution.py:20
  37.3 0.6 dynamic_slice.41
  38.5 0.7 collective-permute-done
  39.2 0.4 collective-permute-done.1
  39.5 1.4 %conditional.4 = (f32[128,7,128]{2,0,1:T(8,128)S(1)}, f32[128,128]{1,0:T(8,128)S(1)}, f32[128,128]{1,0:T(8,128)S(1)}) conditional(s32[]{:T(128)} %bitcast.101, () %tuple.83, (s32[]{:T(128)}, s32[1024]{0:T(1024)S(1)}, s32[128]{0:T(128)S(1)}, bf16[128,128]{1,0:T(8,128)(2,1)S(1)}, bf16[128,7,128]{2,0,1:T(8,128)(2,1)S(1)}, ...), branch_computations={%region_4.4_spmd, %region_5.5_spmd} | conditional | flops 147636352 | bytes 3712330 | solution.py:100
  40.2 0.3 convolution_bitcast_fusion.4
  41.5 3.4 %collective-permute-start.1 = (bf16[128,128]{1,0:T(8,128)(2,1)S(1)}, bf16[128,128]{1,0:T(8,128)(2,1)S(1)}, u32[]{:S(2)}, u32[]{:S(2)}) collective-permute-start(bf16[128,128]{1,0:T(8,128)(2,1)S(1)} %get-tuple-element.706), channel_id=1, source_target_pairs={{0,1},{1,2},{2,3},{3,4},{4,5},{5,6},{6,7},{7,0},{8,9},{9,10},{10,1... | collective-permute-start | bytes 98312 | tf_op jit(solution)/shard_map/while/body/eval_jaxpr/ppermute | solution.py:20
  44.9 0.6 dynamic_slice.41
  46.1 0.7 collective-permute-done
  46.8 0.4 collective-permute-done.1
  47.2 1.4 %conditional.4 = (f32[128,7,128]{2,0,1:T(8,128)S(1)}, f32[128,128]{1,0:T(8,128)S(1)}, f32[128,128]{1,0:T(8,128)S(1)}) conditional(s32[]{:T(128)} %bitcast.101, () %tuple.83, (s32[]{:T(128)}, s32[1024]{0:T(1024)S(1)}, s32[128]{0:T(128)S(1)}, bf16[128,128]{1,0:T(8,128)(2,1)S(1)}, bf16[128,7,128]{2,0,1:T(8,128)(2,1)S(1)}, ...), branch_computations={%region_4.4_spmd, %region_5.5_spmd} | conditional | flops 147636352 | bytes 3712330 | solution.py:100
  47.4 0.2 fusion.15
  47.9 0.3 convolution_bitcast_fusion.4
  49.0 3.6 %collective-permute-start.1 = (bf16[128,128]{1,0:T(8,128)(2,1)S(1)}, bf16[128,128]{1,0:T(8,128)(2,1)S(1)}, u32[]{:S(2)}, u32[]{:S(2)}) collective-permute-start(bf16[128,128]{1,0:T(8,128)(2,1)S(1)} %get-tuple-element.706), channel_id=1, source_target_pairs={{0,1},{1,2},{2,3},{3,4},{4,5},{5,6},{6,7},{7,0},{8,9},{9,10},{10,1... | collective-permute-start | bytes 98312 | tf_op jit(solution)/shard_map/while/body/eval_jaxpr/ppermute | solution.py:20
  52.5 0.6 dynamic_slice.41
  53.8 0.7 collective-permute-done
  54.5 0.4 collective-permute-done.1
  54.8 1.4 %conditional.4 = (f32[128,7,128]{2,0,1:T(8,128)S(1)}, f32[128,128]{1,0:T(8,128)S(1)}, f32[128,128]{1,0:T(8,128)S(1)}) conditional(s32[]{:T(128)} %bitcast.101, () %tuple.83, (s32[]{:T(128)}, s32[1024]{0:T(1024)S(1)}, s32[128]{0:T(128)S(1)}, bf16[128,128]{1,0:T(8,128)(2,1)S(1)}, bf16[128,7,128]{2,0,1:T(8,128)(2,1)S(1)}, ...), branch_computations={%region_4.4_spmd, %region_5.5_spmd} | conditional | flops 147636352 | bytes 3712330 | solution.py:100
  55.5 0.3 convolution_bitcast_fusion.4
  56.5 1.4 %collective-permute-start.2 = (f32[128,128]{1,0:T(8,128)S(1)}, f32[128,128]{1,0:T(8,128)S(1)}, u32[]{:S(2)}, u32[]{:S(2)}) collective-permute-start(f32[128,128]{1,0:T(8,128)S(1)} %get-tuple-element.707), channel_id=1, source_target_pairs={{0,1},{1,2},{2,3},{3,4},{4,5},{5,6},{6,7},{7,0},{8,9},{9,10},{10,1... | collective-permute-start | bytes 196616 | tf_op jit(solution)/shard_map/while/body/eval_jaxpr/ppermute | solution.py:20
  58.0 0.9 collective-permute-start.1
  58.9 0.6 dynamic_slice.41
  60.1 2.0 %collective-permute-done = bf16[128,128]{1,0:T(8,128)(2,1)S(1)} collective-permute-done((bf16[128,128]{1,0:T(8,128)(2,1)S(1)}, bf16[128,128]{1,0:T(8,128)(2,1)S(1)}, u32[]{:S(2)}, u32[]{:S(2)}) %collective-permute-start) | collective-permute-done | bytes 32800 | tf_op jit(solution)/shard_map/while/body/eval_jaxpr/ppermute | solution.py:20
  62.1 0.4 collective-permute-done.1
  62.5 1.4 %conditional.4 = (f32[128,7,128]{2,0,1:T(8,128)S(1)}, f32[128,128]{1,0:T(8,128)S(1)}, f32[128,128]{1,0:T(8,128)S(1)}) conditional(s32[]{:T(128)} %bitcast.101, () %tuple.83, (s32[]{:T(128)}, s32[1024]{0:T(1024)S(1)}, s32[128]{0:T(128)S(1)}, bf16[128,128]{1,0:T(8,128)(2,1)S(1)}, bf16[128,7,128]{2,0,1:T(8,128)(2,1)S(1)}, ...), branch_computations={%region_4.4_spmd, %region_5.5_spmd} | conditional | flops 147636352 | bytes 3712330 | solution.py:100
  63.2 0.3 convolution_bitcast_fusion.4
  64.1 0.5 collective-permute-start.2
  64.7 0.5 collective-permute-start.1
  65.2 0.6 dynamic_slice.41
  66.4 3.3 %collective-permute-done = bf16[128,128]{1,0:T(8,128)(2,1)S(1)} collective-permute-done((bf16[128,128]{1,0:T(8,128)(2,1)S(1)}, bf16[128,128]{1,0:T(8,128)(2,1)S(1)}, u32[]{:S(2)}, u32[]{:S(2)}) %collective-permute-start) | collective-permute-done | bytes 32800 | tf_op jit(solution)/shard_map/while/body/eval_jaxpr/ppermute | solution.py:20
  69.8 0.4 collective-permute-done.1
  70.1 1.4 %conditional.4 = (f32[128,7,128]{2,0,1:T(8,128)S(1)}, f32[128,128]{1,0:T(8,128)S(1)}, f32[128,128]{1,0:T(8,128)S(1)}) conditional(s32[]{:T(128)} %bitcast.101, () %tuple.83, (s32[]{:T(128)}, s32[1024]{0:T(1024)S(1)}, s32[128]{0:T(128)S(1)}, bf16[128,128]{1,0:T(8,128)(2,1)S(1)}, bf16[128,7,128]{2,0,1:T(8,128)(2,1)S(1)}, ...), branch_computations={%region_4.4_spmd, %region_5.5_spmd} | conditional | flops 147636352 | bytes 3712330 | solution.py:100
  70.8 0.3 convolution_bitcast_fusion.4
  72.8 0.8 copy.29
  73.6 2.7 %collective-permute-done.4 = f32[128,128]{1,0:T(8,128)S(1)} collective-permute-done((f32[128,128]{1,0:T(8,128)S(1)}, f32[128,128]{1,0:T(8,128)S(1)}, u32[]{:S(2)}, u32[]{:S(2)}) %collective-permute-start.4) | collective-permute-done | bytes 65568 | tf_op jit(solution)/shard_map/ppermute | solution.py:20
  76.4 0.3 fusion.29
  76.8 0.3 dynamic_update_slice.10
  77.1 0.7 convert_bitcast_fusion.1
  77.8 0.6 fusion.32
  78.6 40.0 %psum.7 = f32[4608]{0:T(1024)} all-reduce(f32[4608]{0:T(1024)S(1)} %dynamic_update_slice.11), channel_id=1, replica_groups=mesh['outer'=4,'inner'=8] {'outer','inner'}, use_global_device_ids=true, to_apply=%region_10.11 | all-reduce | flops 4608 | bytes 36864 | tf_op jit(solution)/shard_map/psum | solution.py:141
  (138 shorter events, 10.7 us)
Async XLA Ops:
  0.6 0.8 copy-start.2
  1.4 1.2 copy-start
  2.9 0.9 copy-start.1
  3.9 0.7 copy-start.3
  14.7 0.7 copy-start.5
  16.6 0.7 copy-start.4
  18.7 6.5 %collective-permute-start.3 = (f32[128,128]{1,0:T(8,128)S(1)}, f32[128,128]{1,0:T(8,128)S(1)}, u32[]{:S(2)}, u32[]{:S(2)}) collective-permute-start(f32[128,128]{1,0:T(8,128)S(1)} %get-tuple-element.708), channel_id=1, source_target_pairs={{0,1},{1,2},{2,3},{3,4},{4,5},{5,6},{6,7},{7,0},{8,9},{9,10},{10,1... | collective-permute-start | bytes 196616 | tf_op jit(solution)/shard_map/while/body/eval_jaxpr/ppermute | solution.py:20
  19.1 6.1 %collective-permute-start.2 = (f32[128,128]{1,0:T(8,128)S(1)}, f32[128,128]{1,0:T(8,128)S(1)}, u32[]{:S(2)}, u32[]{:S(2)}) collective-permute-start(f32[128,128]{1,0:T(8,128)S(1)} %get-tuple-element.707), channel_id=1, source_target_pairs={{0,1},{1,2},{2,3},{3,4},{4,5},{5,6},{6,7},{7,0},{8,9},{9,10},{10,1... | collective-permute-start | bytes 196616 | tf_op jit(solution)/shard_map/while/body/eval_jaxpr/ppermute | solution.py:20
  20.4 4.2 %collective-permute-start = (bf16[128,128]{1,0:T(8,128)(2,1)S(1)}, bf16[128,128]{1,0:T(8,128)(2,1)S(1)}, u32[]{:S(2)}, u32[]{:S(2)}) collective-permute-start(bf16[128,128]{1,0:T(8,128)(2,1)S(1)} %get-tuple-element.705), channel_id=1, source_target_pairs={{0,1},{1,2},{2,3},{3,4},{4,5},{5,6},{6,7},{7,0},{8,9},{9,10},{10,1... | collective-permute-start | bytes 98312 | tf_op jit(solution)/shard_map/while/body/eval_jaxpr/ppermute | solution.py:20
  20.7 4.3 %collective-permute-start.1 = (bf16[128,128]{1,0:T(8,128)(2,1)S(1)}, bf16[128,128]{1,0:T(8,128)(2,1)S(1)}, u32[]{:S(2)}, u32[]{:S(2)}) collective-permute-start(bf16[128,128]{1,0:T(8,128)(2,1)S(1)} %get-tuple-element.706), channel_id=1, source_target_pairs={{0,1},{1,2},{2,3},{3,4},{4,5},{5,6},{6,7},{7,0},{8,9},{9,10},{10,1... | collective-permute-start | bytes 98312 | tf_op jit(solution)/shard_map/while/body/eval_jaxpr/ppermute | solution.py:20
  25.3 6.8 %collective-permute-start.3 = (f32[128,128]{1,0:T(8,128)S(1)}, f32[128,128]{1,0:T(8,128)S(1)}, u32[]{:S(2)}, u32[]{:S(2)}) collective-permute-start(f32[128,128]{1,0:T(8,128)S(1)} %get-tuple-element.708), channel_id=1, source_target_pairs={{0,1},{1,2},{2,3},{3,4},{4,5},{5,6},{6,7},{7,0},{8,9},{9,10},{10,1... | collective-permute-start | bytes 196616 | tf_op jit(solution)/shard_map/while/body/eval_jaxpr/ppermute | solution.py:20
  25.3 6.8 %collective-permute-start.2 = (f32[128,128]{1,0:T(8,128)S(1)}, f32[128,128]{1,0:T(8,128)S(1)}, u32[]{:S(2)}, u32[]{:S(2)}) collective-permute-start(f32[128,128]{1,0:T(8,128)S(1)} %get-tuple-element.707), channel_id=1, source_target_pairs={{0,1},{1,2},{2,3},{3,4},{4,5},{5,6},{6,7},{7,0},{8,9},{9,10},{10,1... | collective-permute-start | bytes 196616 | tf_op jit(solution)/shard_map/while/body/eval_jaxpr/ppermute | solution.py:20
  27.3 4.2 %collective-permute-start = (bf16[128,128]{1,0:T(8,128)(2,1)S(1)}, bf16[128,128]{1,0:T(8,128)(2,1)S(1)}, u32[]{:S(2)}, u32[]{:S(2)}) collective-permute-start(bf16[128,128]{1,0:T(8,128)(2,1)S(1)} %get-tuple-element.705), channel_id=1, source_target_pairs={{0,1},{1,2},{2,3},{3,4},{4,5},{5,6},{6,7},{7,0},{8,9},{9,10},{10,1... | collective-permute-start | bytes 98312 | tf_op jit(solution)/shard_map/while/body/eval_jaxpr/ppermute | solution.py:20
  27.4 4.5 %collective-permute-start.1 = (bf16[128,128]{1,0:T(8,128)(2,1)S(1)}, bf16[128,128]{1,0:T(8,128)(2,1)S(1)}, u32[]{:S(2)}, u32[]{:S(2)}) collective-permute-start(bf16[128,128]{1,0:T(8,128)(2,1)S(1)} %get-tuple-element.706), channel_id=1, source_target_pairs={{0,1},{1,2},{2,3},{3,4},{4,5},{5,6},{6,7},{7,0},{8,9},{9,10},{10,1... | collective-permute-start | bytes 98312 | tf_op jit(solution)/shard_map/while/body/eval_jaxpr/ppermute | solution.py:20
  32.2 8.9 %collective-permute-start.3 = (f32[128,128]{1,0:T(8,128)S(1)}, f32[128,128]{1,0:T(8,128)S(1)}, u32[]{:S(2)}, u32[]{:S(2)}) collective-permute-start(f32[128,128]{1,0:T(8,128)S(1)} %get-tuple-element.708), channel_id=1, source_target_pairs={{0,1},{1,2},{2,3},{3,4},{4,5},{5,6},{6,7},{7,0},{8,9},{9,10},{10,1... | collective-permute-start | bytes 196616 | tf_op jit(solution)/shard_map/while/body/eval_jaxpr/ppermute | solution.py:20
  32.2 8.9 %collective-permute-start.2 = (f32[128,128]{1,0:T(8,128)S(1)}, f32[128,128]{1,0:T(8,128)S(1)}, u32[]{:S(2)}, u32[]{:S(2)}) collective-permute-start(f32[128,128]{1,0:T(8,128)S(1)} %get-tuple-element.707), channel_id=1, source_target_pairs={{0,1},{1,2},{2,3},{3,4},{4,5},{5,6},{6,7},{7,0},{8,9},{9,10},{10,1... | collective-permute-start | bytes 196616 | tf_op jit(solution)/shard_map/while/body/eval_jaxpr/ppermute | solution.py:20
  34.9 4.2 %collective-permute-start = (bf16[128,128]{1,0:T(8,128)(2,1)S(1)}, bf16[128,128]{1,0:T(8,128)(2,1)S(1)}, u32[]{:S(2)}, u32[]{:S(2)}) collective-permute-start(bf16[128,128]{1,0:T(8,128)(2,1)S(1)} %get-tuple-element.705), channel_id=1, source_target_pairs={{0,1},{1,2},{2,3},{3,4},{4,5},{5,6},{6,7},{7,0},{8,9},{9,10},{10,1... | collective-permute-start | bytes 98312 | tf_op jit(solution)/shard_map/while/body/eval_jaxpr/ppermute | solution.py:20
  35.0 4.5 %collective-permute-start.1 = (bf16[128,128]{1,0:T(8,128)(2,1)S(1)}, bf16[128,128]{1,0:T(8,128)(2,1)S(1)}, u32[]{:S(2)}, u32[]{:S(2)}) collective-permute-start(bf16[128,128]{1,0:T(8,128)(2,1)S(1)} %get-tuple-element.706), channel_id=1, source_target_pairs={{0,1},{1,2},{2,3},{3,4},{4,5},{5,6},{6,7},{7,0},{8,9},{9,10},{10,1... | collective-permute-start | bytes 98312 | tf_op jit(solution)/shard_map/while/body/eval_jaxpr/ppermute | solution.py:20
  41.1 7.6 %collective-permute-start.3 = (f32[128,128]{1,0:T(8,128)S(1)}, f32[128,128]{1,0:T(8,128)S(1)}, u32[]{:S(2)}, u32[]{:S(2)}) collective-permute-start(f32[128,128]{1,0:T(8,128)S(1)} %get-tuple-element.708), channel_id=1, source_target_pairs={{0,1},{1,2},{2,3},{3,4},{4,5},{5,6},{6,7},{7,0},{8,9},{9,10},{10,1... | collective-permute-start | bytes 196616 | tf_op jit(solution)/shard_map/while/body/eval_jaxpr/ppermute | solution.py:20
  41.2 7.5 %collective-permute-start.2 = (f32[128,128]{1,0:T(8,128)S(1)}, f32[128,128]{1,0:T(8,128)S(1)}, u32[]{:S(2)}, u32[]{:S(2)}) collective-permute-start(f32[128,128]{1,0:T(8,128)S(1)} %get-tuple-element.707), channel_id=1, source_target_pairs={{0,1},{1,2},{2,3},{3,4},{4,5},{5,6},{6,7},{7,0},{8,9},{9,10},{10,1... | collective-permute-start | bytes 196616 | tf_op jit(solution)/shard_map/while/body/eval_jaxpr/ppermute | solution.py:20
  41.3 5.6 %collective-permute-start = (bf16[128,128]{1,0:T(8,128)(2,1)S(1)}, bf16[128,128]{1,0:T(8,128)(2,1)S(1)}, u32[]{:S(2)}, u32[]{:S(2)}) collective-permute-start(bf16[128,128]{1,0:T(8,128)(2,1)S(1)} %get-tuple-element.705), channel_id=1, source_target_pairs={{0,1},{1,2},{2,3},{3,4},{4,5},{5,6},{6,7},{7,0},{8,9},{9,10},{10,1... | collective-permute-start | bytes 98312 | tf_op jit(solution)/shard_map/while/body/eval_jaxpr/ppermute | solution.py:20
  41.5 5.7 %collective-permute-start.1 = (bf16[128,128]{1,0:T(8,128)(2,1)S(1)}, bf16[128,128]{1,0:T(8,128)(2,1)S(1)}, u32[]{:S(2)}, u32[]{:S(2)}) collective-permute-start(bf16[128,128]{1,0:T(8,128)(2,1)S(1)} %get-tuple-element.706), channel_id=1, source_target_pairs={{0,1},{1,2},{2,3},{3,4},{4,5},{5,6},{6,7},{7,0},{8,9},{9,10},{10,1... | collective-permute-start | bytes 98312 | tf_op jit(solution)/shard_map/while/body/eval_jaxpr/ppermute | solution.py:20
  48.8 7.6 %collective-permute-start.3 = (f32[128,128]{1,0:T(8,128)S(1)}, f32[128,128]{1,0:T(8,128)S(1)}, u32[]{:S(2)}, u32[]{:S(2)}) collective-permute-start(f32[128,128]{1,0:T(8,128)S(1)} %get-tuple-element.708), channel_id=1, source_target_pairs={{0,1},{1,2},{2,3},{3,4},{4,5},{5,6},{6,7},{7,0},{8,9},{9,10},{10,1... | collective-permute-start | bytes 196616 | tf_op jit(solution)/shard_map/while/body/eval_jaxpr/ppermute | solution.py:20
  48.8 7.5 %collective-permute-start.2 = (f32[128,128]{1,0:T(8,128)S(1)}, f32[128,128]{1,0:T(8,128)S(1)}, u32[]{:S(2)}, u32[]{:S(2)}) collective-permute-start(f32[128,128]{1,0:T(8,128)S(1)} %get-tuple-element.707), channel_id=1, source_target_pairs={{0,1},{1,2},{2,3},{3,4},{4,5},{5,6},{6,7},{7,0},{8,9},{9,10},{10,1... | collective-permute-start | bytes 196616 | tf_op jit(solution)/shard_map/while/body/eval_jaxpr/ppermute | solution.py:20
  48.9 5.6 %collective-permute-start = (bf16[128,128]{1,0:T(8,128)(2,1)S(1)}, bf16[128,128]{1,0:T(8,128)(2,1)S(1)}, u32[]{:S(2)}, u32[]{:S(2)}) collective-permute-start(bf16[128,128]{1,0:T(8,128)(2,1)S(1)} %get-tuple-element.705), channel_id=1, source_target_pairs={{0,1},{1,2},{2,3},{3,4},{4,5},{5,6},{6,7},{7,0},{8,9},{9,10},{10,1... | collective-permute-start | bytes 98312 | tf_op jit(solution)/shard_map/while/body/eval_jaxpr/ppermute | solution.py:20
  49.0 5.8 %collective-permute-start.1 = (bf16[128,128]{1,0:T(8,128)(2,1)S(1)}, bf16[128,128]{1,0:T(8,128)(2,1)S(1)}, u32[]{:S(2)}, u32[]{:S(2)}) collective-permute-start(bf16[128,128]{1,0:T(8,128)(2,1)S(1)} %get-tuple-element.706), channel_id=1, source_target_pairs={{0,1},{1,2},{2,3},{3,4},{4,5},{5,6},{6,7},{7,0},{8,9},{9,10},{10,1... | collective-permute-start | bytes 98312 | tf_op jit(solution)/shard_map/while/body/eval_jaxpr/ppermute | solution.py:20
  56.4 7.6 %collective-permute-start.3 = (f32[128,128]{1,0:T(8,128)S(1)}, f32[128,128]{1,0:T(8,128)S(1)}, u32[]{:S(2)}, u32[]{:S(2)}) collective-permute-start(f32[128,128]{1,0:T(8,128)S(1)} %get-tuple-element.708), channel_id=1, source_target_pairs={{0,1},{1,2},{2,3},{3,4},{4,5},{5,6},{6,7},{7,0},{8,9},{9,10},{10,1... | collective-permute-start | bytes 196616 | tf_op jit(solution)/shard_map/while/body/eval_jaxpr/ppermute | solution.py:20
  56.5 7.5 %collective-permute-start.2 = (f32[128,128]{1,0:T(8,128)S(1)}, f32[128,128]{1,0:T(8,128)S(1)}, u32[]{:S(2)}, u32[]{:S(2)}) collective-permute-start(f32[128,128]{1,0:T(8,128)S(1)} %get-tuple-element.707), channel_id=1, source_target_pairs={{0,1},{1,2},{2,3},{3,4},{4,5},{5,6},{6,7},{7,0},{8,9},{9,10},{10,1... | collective-permute-start | bytes 196616 | tf_op jit(solution)/shard_map/while/body/eval_jaxpr/ppermute | solution.py:20
  57.9 4.2 %collective-permute-start = (bf16[128,128]{1,0:T(8,128)(2,1)S(1)}, bf16[128,128]{1,0:T(8,128)(2,1)S(1)}, u32[]{:S(2)}, u32[]{:S(2)}) collective-permute-start(bf16[128,128]{1,0:T(8,128)(2,1)S(1)} %get-tuple-element.705), channel_id=1, source_target_pairs={{0,1},{1,2},{2,3},{3,4},{4,5},{5,6},{6,7},{7,0},{8,9},{9,10},{10,1... | collective-permute-start | bytes 98312 | tf_op jit(solution)/shard_map/while/body/eval_jaxpr/ppermute | solution.py:20
  58.0 4.5 %collective-permute-start.1 = (bf16[128,128]{1,0:T(8,128)(2,1)S(1)}, bf16[128,128]{1,0:T(8,128)(2,1)S(1)}, u32[]{:S(2)}, u32[]{:S(2)}) collective-permute-start(bf16[128,128]{1,0:T(8,128)(2,1)S(1)} %get-tuple-element.706), channel_id=1, source_target_pairs={{0,1},{1,2},{2,3},{3,4},{4,5},{5,6},{6,7},{7,0},{8,9},{9,10},{10,1... | collective-permute-start | bytes 98312 | tf_op jit(solution)/shard_map/while/body/eval_jaxpr/ppermute | solution.py:20
  64.1 7.6 %collective-permute-start.3 = (f32[128,128]{1,0:T(8,128)S(1)}, f32[128,128]{1,0:T(8,128)S(1)}, u32[]{:S(2)}, u32[]{:S(2)}) collective-permute-start(f32[128,128]{1,0:T(8,128)S(1)} %get-tuple-element.708), channel_id=1, source_target_pairs={{0,1},{1,2},{2,3},{3,4},{4,5},{5,6},{6,7},{7,0},{8,9},{9,10},{10,1... | collective-permute-start | bytes 196616 | tf_op jit(solution)/shard_map/while/body/eval_jaxpr/ppermute | solution.py:20
  64.1 7.5 %collective-permute-start.2 = (f32[128,128]{1,0:T(8,128)S(1)}, f32[128,128]{1,0:T(8,128)S(1)}, u32[]{:S(2)}, u32[]{:S(2)}) collective-permute-start(f32[128,128]{1,0:T(8,128)S(1)} %get-tuple-element.707), channel_id=1, source_target_pairs={{0,1},{1,2},{2,3},{3,4},{4,5},{5,6},{6,7},{7,0},{8,9},{9,10},{10,1... | collective-permute-start | bytes 196616 | tf_op jit(solution)/shard_map/while/body/eval_jaxpr/ppermute | solution.py:20
  64.6 5.1 %collective-permute-start = (bf16[128,128]{1,0:T(8,128)(2,1)S(1)}, bf16[128,128]{1,0:T(8,128)(2,1)S(1)}, u32[]{:S(2)}, u32[]{:S(2)}) collective-permute-start(bf16[128,128]{1,0:T(8,128)(2,1)S(1)} %get-tuple-element.705), channel_id=1, source_target_pairs={{0,1},{1,2},{2,3},{3,4},{4,5},{5,6},{6,7},{7,0},{8,9},{9,10},{10,1... | collective-permute-start | bytes 98312 | tf_op jit(solution)/shard_map/while/body/eval_jaxpr/ppermute | solution.py:20
  64.7 5.4 %collective-permute-start.1 = (bf16[128,128]{1,0:T(8,128)(2,1)S(1)}, bf16[128,128]{1,0:T(8,128)(2,1)S(1)}, u32[]{:S(2)}, u32[]{:S(2)}) collective-permute-start(bf16[128,128]{1,0:T(8,128)(2,1)S(1)} %get-tuple-element.706), channel_id=1, source_target_pairs={{0,1},{1,2},{2,3},{3,4},{4,5},{5,6},{6,7},{7,0},{8,9},{9,10},{10,1... | collective-permute-start | bytes 98312 | tf_op jit(solution)/shard_map/while/body/eval_jaxpr/ppermute | solution.py:20
  71.7 4.6 %collective-permute-start.4 = (f32[128,128]{1,0:T(8,128)S(1)}, f32[128,128]{1,0:T(8,128)S(1)}, u32[]{:S(2)}, u32[]{:S(2)}) collective-permute-start(f32[128,128]{1,0:T(8,128)S(1)} %get-tuple-element.490), channel_id=1, source_target_pairs={{0,1},{1,2},{2,3},{3,4},{4,5},{5,6},{6,7},{7,0},{8,9},{9,10},{10,1... | collective-permute-start | bytes 196616 | tf_op jit(solution)/shard_map/ppermute | solution.py:20
  71.8 6.0 %collective-permute-start.5 = (f32[128,128]{1,0:T(8,128)S(1)}, f32[128,128]{1,0:T(8,128)S(1)}, u32[]{:S(2)}, u32[]{:S(2)}) collective-permute-start(f32[128,128]{1,0:T(8,128)S(1)} %get-tuple-element.491), channel_id=1, source_target_pairs={{0,1},{1,2},{2,3},{3,4},{4,5},{5,6},{6,7},{7,0},{8,9},{9,10},{10,1... | collective-permute-start | bytes 196616 | tf_op jit(solution)/shard_map/ppermute | solution.py:20
where the time goes:
time: 119 us
  blocking collectives  50.2 us (42%)
  starting transfers between devices  23.8 us (20%)
  waiting for transfers between devices  14.8 us (12%)
  local copies, waits for them, and re-layouts  10.9 us (9%)
  matrix products  7.05 us (6%)
  loops' own time  5.4 us (5%)
  other arithmetic  4.9 us (4%)
  between operations  1.49 us (1%)
    psum x1, blocking collectives, local(): grad_bias = lax.psum(bias_local, ('outer', 'inner'))  40 us
    ppermute x30, starting transfers between devices, passed_along(): return lax.ppermute(value, axis, pairs)  23.8 us
    ppermute x30, waiting for transfers between devices, passed_along(): return lax.ppermute(value, axis, pairs)  14.8 us
    all_gather x1, blocking collectives, local(): seg_every = lax.all_gather(segments, 'inner', axis=1, tiled=True)  10.2 us
    unnamed x18, local copies, waits for them, and re-layouts  5.59 us
    another operation x1, loops' own time, local(): lax.fori_loop(1, members, one_turn, (own_pair, (own_key, own_value), own_...  5.15 us
    dynamic_slice x7, local copies, waits for them, and re-layouts, contribution(): return lax.cond(table_row[source] > 0, compute, nothing, 0)  4.07 us
  transfers between devices with their start and end apart: 30, of which 15 were waited for; matrix products, arithmetic and copies ran while one was open for 13% of the time, Pallas kernels for 0%

commit v1 on v0

v1 whole, which is shorter than its diff:
```python
import functools
import math

import jax
import jax.numpy as jnp
from jax import lax
from jax.experimental import pallas as pl
from jax.experimental.pallas import tpu as pltpu
from jax.sharding import PartitionSpec as P

HEADS = 28
KV_HEADS = 4
HEAD_DIM = 128
GROUP = HEADS // KV_HEADS
ROPE_BASE = 1000000.0
ROOT = math.sqrt(HEAD_DIM)
SCALE = 1.0 / ROOT
EXP2_SCALE = math.log2(math.e) / ROOT
MASKED = -1e30
EXTRA = 16
BIAS_ROWS = 16
MESH = pl.DeviceIdType.MESH
F32 = jnp.float32
BF16 = jnp.bfloat16


def partner(index, step, count):
    result = 0
    bit = 1
    while bit < count:
        result = result + ((index // bit + step // bit) % 2) * bit
        bit *= 2
    return result


def pieces(x):
    high = x.astype(BF16).astype(F32)
    rest = x - high
    middle = rest.astype(BF16).astype(F32)
    return high, middle, rest - middle


def dot(a, b):
    return jnp.dot(a, b, preferred_element_type=F32)


def kernel(
    inners, outers, q_ref, k_ref, v_ref, ao_ref, go_ref, norm_ref, seg_ref,
    dq_ref, dk_ref, dv_ref, bias_ref,
    kv, q_aug, go_aug, q_t, go_t, probs, grads, dq_acc, own_acc, part_out, part_in,
    bias_own, bias_in, plane_own, plane_in,
    kv_send, kv_recv, part_send, part_recv, bias_send, bias_recv, plane_send, plane_recv,
):
    tokens = k_ref.shape[0]
    rows = GROUP * tokens
    me = lax.axis_index("inner")
    plane = lax.axis_index("outer")

    def inner_id(step):
        return (plane, partner(me, step, inners))

    def outer_id(step):
        return (partner(plane, step, outers), me)

    barrier = pltpu.get_barrier_semaphore()
    for step in range(1, inners):
        pl.semaphore_signal(barrier, inc=1, device_id=inner_id(step), device_id_type=MESH)
    for step in range(1, outers):
        pl.semaphore_signal(barrier, inc=1, device_id=outer_id(step), device_id_type=MESH)

    seg = seg_ref[...].astype(F32)
    row = lax.broadcasted_iota(jnp.int32, (EXTRA, tokens), 0)
    seg_rows = jnp.broadcast_to(seg, (EXTRA, tokens))
    extra = jnp.where(row < 3, 1.0, 0.0)
    extra = jnp.where((row == 3) & (seg_rows == 1.0), 1.0, extra)
    extra = jnp.where((row == 4) & (seg_rows == 2.0), 1.0, extra)
    kv[0, :HEAD_DIM] = jnp.transpose(v_ref[...])
    kv[0, HEAD_DIM : 2 * HEAD_DIM] = jnp.transpose(k_ref[...])
    kv[0, 2 * HEAD_DIM : 2 * HEAD_DIM + EXTRA] = extra.astype(BF16)
    for slot in range(inners):
        kv[slot, 2 * HEAD_DIM + EXTRA :] = jnp.zeros((HEAD_DIM - EXTRA, tokens), BF16)

    pl.semaphore_wait(barrier, inners + outers - 2)

    sent = 2 * HEAD_DIM + EXTRA

    def kv_copy(step):
        return pltpu.make_async_remote_copy(
            src_ref=kv.at[0, pl.ds(0, sent)],
            dst_ref=kv.at[step, pl.ds(0, sent)],
            send_sem=kv_send.at[step],
            recv_sem=kv_recv.at[step],
            device_id=inner_id(step),
            device_id_type=MESH,
        )

    def part_copy(step):
        return pltpu.make_async_remote_copy(
            src_ref=part_out.at[step],
            dst_ref=part_in.at[step],
            send_sem=part_send.at[step],
            recv_sem=part_recv.at[step],
            device_id=inner_id(step),
            device_id_type=MESH,
        )

    for step in range(1, inners):
        kv_copy(step).start()

    norms = norm_ref[...] * -ROOT
    high, middle, low = pieces(norms)
    row8 = lax.broadcasted_iota(jnp.int32, (8, tokens), 0)
    seg8 = jnp.broadcast_to(seg, (8, tokens))
    masks = jnp.where((row8 == 3) & (seg8 != 1.0), MASKED, 0.0)
    masks = jnp.where((row8 == 4) & (seg8 != 2.0), MASKED, masks)
    lane = lax.broadcasted_iota(jnp.int32, (tokens, HEAD_DIM), 1)
    for g in range(GROUP):
        here = slice(g * tokens, (g + 1) * tokens)
        cols = slice(g * HEAD_DIM, (g + 1) * HEAD_DIM)
        query = q_ref[:, cols]
        grad = go_ref[:, cols]
        q_aug[here, :HEAD_DIM] = query
        go_aug[here, :HEAD_DIM] = grad
        q_t[:, here] = jnp.transpose(query)
        go_t[:, here] = jnp.transpose(grad)
        top = jnp.where(row8 == 0, high[g : g + 1], masks)
        top = jnp.where(row8 == 1, middle[g : g + 1], top)
        top = jnp.where(row8 == 2, low[g : g + 1], top)
        full = jnp.concatenate([top, jnp.zeros((HEAD_DIM - 8, tokens), F32)], axis=0)
        q_aug[here, HEAD_DIM:] = jnp.transpose(full).astype(BF16)
        delta = -jnp.sum(
            grad.astype(F32) * ao_ref[:, cols].astype(F32), axis=1, keepdims=True
        )
        d_high, d_middle, d_low = pieces(delta)
        side = jnp.where(lane == 0, d_high, 0.0)
        side = jnp.where(lane == 1, d_middle, side)
        side = jnp.where(lane == 2, d_low, side)
        go_aug[here, HEAD_DIM:] = side.astype(BF16)

    half = HEAD_DIM // 2
    spot = lax.broadcasted_iota(jnp.int32, (tokens, HEAD_DIM), 0) + me * tokens
    frequency = jnp.exp((lane % half).astype(F32) * (-2.0 * math.log(ROPE_BASE) / HEAD_DIM))
    waves = jnp.sin(spot.astype(F32) * frequency + jnp.where(lane < half, 0.0, math.pi / 2))
    turned = pltpu.roll(waves, half, 1)
    cosine = jnp.where(lane < half, turned, waves)
    sine = jnp.where(lane < half, waves, -turned)

    def unrotate(x):
        return x * cosine + pltpu.roll(x, half, 1) * sine

    chunk = 256
    starts = list(range(0, rows, chunk))

    def compute(g, first):
        block = jnp.concatenate([kv[2 * g], kv[2 * g + 1]], axis=1)
        values_t = jnp.concatenate([block[:HEAD_DIM], block[2 * HEAD_DIM :]], axis=0)
        keys_t = block[HEAD_DIM:]
        keys = jnp.transpose(block[HEAD_DIM : 2 * HEAD_DIM])
        for start in starts:
            here = slice(start, min(start + chunk, rows))
            scores = dot(q_aug[here], keys_t)
            chances = jnp.exp2(scores * EXP2_SCALE)
            probs[here] = chances.astype(BF16)
            low_grads = (chances * dot(go_aug[here], values_t)).astype(BF16)
            grads[here] = low_grads
            part = dot(low_grads, keys)
            if first:
                dq_acc[here] = part
            else:
                dq_acc[here] += part
        value_part = dot(go_t[...], probs[...])
        key_part = dot(q_t[...], grads[...])
        return key_part, value_part

    def put(slot, key_part, value_part):
        part_out[slot, :HEAD_DIM] = key_part.astype(BF16)
        part_out[slot, HEAD_DIM:] = value_part.astype(BF16)
        part_copy(slot).start()

    kv_copy(1).wait_recv()
    key_part, value_part = compute(0, True)
    own_acc[:HEAD_DIM] = key_part[:, :tokens]
    own_acc[HEAD_DIM:] = value_part[:, :tokens]
    put(1, key_part[:, tokens:], value_part[:, tokens:])

    def turn(g, carry):
        kv_copy(2 * g).wait_recv()
        kv_copy(2 * g + 1).wait_recv()
        key_part, value_part = compute(g, False)
        put(2 * g, key_part[:, :tokens], value_part[:, :tokens])
        put(2 * g + 1, key_part[:, tokens:], value_part[:, tokens:])
        return carry

    groups = inners // 2
    if groups <= 4:
        for g in range(1, groups):
            turn(g, 0)
    else:
        lax.fori_loop(1, groups, turn, 0)

    bias_own[...] = jnp.zeros((BIAS_ROWS, HEAD_DIM), F32)
    for g in range(GROUP):
        full = unrotate(dq_acc[g * tokens : (g + 1) * tokens] * SCALE)
        dq_ref[:, g * HEAD_DIM : (g + 1) * HEAD_DIM] = full.astype(BF16)
        bias_own[g : g + 1] = jnp.sum(full, axis=0, keepdims=True)

    total = own_acc[...]
    for step in range(1, inners):
        part_copy(step).wait_recv()
        total = total + part_in[step].astype(F32)
    key_full = unrotate(jnp.transpose(total[:HEAD_DIM]) * SCALE)
    value_full = jnp.transpose(total[HEAD_DIM:])
    dk_ref[...] = key_full.astype(BF16)
    dv_ref[...] = value_full.astype(BF16)
    bias_own[GROUP : GROUP + 1] = jnp.sum(key_full, axis=0, keepdims=True)
    bias_own[GROUP + 1 : GROUP + 2] = jnp.sum(value_full, axis=0, keepdims=True)

    def bias_copy(step, slot):
        return pltpu.make_async_remote_copy(
            src_ref=bias_own,
            dst_ref=bias_in.at[slot],
            send_sem=bias_send.at[step],
            recv_sem=bias_recv.at[step],
            device_id=inner_id(step),
            device_id_type=MESH,
        )

    def plane_copy(step, slot):
        return pltpu.make_async_remote_copy(
            src_ref=plane_own,
            dst_ref=plane_in.at[slot],
            send_sem=plane_send.at[step],
            recv_sem=plane_recv.at[step],
            device_id=outer_id(step),
            device_id_type=MESH,
        )

    for step in range(1, inners):
        bias_copy(step, me).start()
    bias_in[me] = bias_own[...]
    for step in range(1, inners):
        bias_copy(step, partner(me, step, inners)).wait_recv()
    summed = bias_in[0]
    for slot in range(1, inners):
        summed = summed + bias_in[slot]
    plane_own[...] = summed
    for step in range(1, outers):
        plane_copy(step, plane).start()
    plane_in[plane] = summed
    for step in range(1, outers):
        plane_copy(step, partner(plane, step, outers)).wait_recv()
    for head in range(KV_HEADS):
        whole = plane_in[head]
        for other in range(head + KV_HEADS, outers, KV_HEADS):
            whole = whole + plane_in[other]
        bias_ref[head * GROUP : (head + 1) * GROUP] = whole[:GROUP]
        bias_ref[HEADS + head : HEADS + head + 1] = whole[GROUP : GROUP + 1]
        at = HEADS + KV_HEADS + head
        bias_ref[at : at + 1] = whole[GROUP + 1 : GROUP + 2]

    for step in range(1, inners):
        kv_copy(step).wait_send()
        part_copy(step).wait_send()
        bias_copy(step, me).wait_send()
    for step in range(1, outers):
        plane_copy(step, plane).wait_send()


def local(inners, outers, query_rot, key_rot, value_rows, attention_out, grad_out, log_norm,
          segments, block_table):
    del block_table
    tokens = query_rot.shape[1]
    rows = GROUP * tokens
    if segments.shape[0] > 1:
        example = lax.axis_index("outer") // KV_HEADS
        segments = lax.dynamic_slice_in_dim(segments, example, 1, 0)
    vmem = pl.BlockSpec(memory_space=pltpu.VMEM)
    sems = pltpu.SemaphoreType.DMA
    outs = pl.pallas_call(
        functools.partial(kernel, inners, outers),
        out_shape=(
            jax.ShapeDtypeStruct((tokens, GROUP * HEAD_DIM), BF16),
            jax.ShapeDtypeStruct((tokens, HEAD_DIM), BF16),
            jax.ShapeDtypeStruct((tokens, HEAD_DIM), BF16),
            jax.ShapeDtypeStruct((HEADS + 2 * KV_HEADS, HEAD_DIM), F32),
        ),
        in_specs=[vmem] * 7,
        out_specs=(vmem,) * 4,
        scratch_shapes=[
            pltpu.VMEM((inners, 3 * HEAD_DIM, tokens), BF16),
            pltpu.VMEM((rows, 2 * HEAD_DIM), BF16),
            pltpu.VMEM((rows, 2 * HEAD_DIM), BF16),
            pltpu.VMEM((HEAD_DIM, rows), BF16),
            pltpu.VMEM((HEAD_DIM, rows), BF16),
            pltpu.VMEM((rows, 2 * tokens), BF16),
            pltpu.VMEM((rows, 2 * tokens), BF16),
            pltpu.VMEM((rows, HEAD_DIM), F32),
            pltpu.VMEM((2 * HEAD_DIM, tokens), F32),
            pltpu.VMEM((inners, 2 * HEAD_DIM, tokens), BF16),
            pltpu.VMEM((inners, 2 * HEAD_DIM, tokens), BF16),
            pltpu.VMEM((BIAS_ROWS, HEAD_DIM), F32),
            pltpu.VMEM((inners, BIAS_ROWS, HEAD_DIM), F32),
            pltpu.VMEM((BIAS_ROWS, HEAD_DIM), F32),
            pltpu.VMEM((outers, BIAS_ROWS, HEAD_DIM), F32),
            sems((inners,)), sems((inners,)), sems((inners,)), sems((inners,)),
            sems((inners,)), sems((inners,)), sems((outers,)), sems((outers,)),
        ],
        compiler_params=pltpu.CompilerParams(
            collective_id=0, has_side_effects=True, vmem_limit_bytes=48 * 1024 * 1024
        ),
        name="attention_backward",
    )(query_rot[0], key_rot[0], value_rows[0], attention_out[0], grad_out[0], log_norm[0], segments)
    return outs[0][None], outs[1][None], outs[2][None], outs[3].reshape(-1)


def solution(mesh):
    placed = (
        P("outer", "inner", None),
        P("outer", "inner", None),
        P("outer", "inner", None),
        P("outer", "inner", None),
        P("outer", "inner", None),
        P("outer", None, "inner"),
        P(None, "inner"),
        P(None, "inner", None),
    )
    return jax.shard_map(
        functools.partial(local, mesh.shape["inner"], mesh.shape["outer"]),
        mesh=mesh,
        in_specs=placed,
        out_specs=(
            P("outer", "inner", None),
            P("outer", "inner", None),
            P("outer", "inner", None),
            P(),
        ),
        check_vma=False,
    )
```

time: 119 us -> 36.9 us (0.31)
  blocking collectives: 50.2 us -> 0 us
  Pallas kernels: 0 us -> 27.6 us
  starting transfers between devices: 23.8 us -> 0 us
  waiting for transfers between devices: 14.8 us -> 0 us
  matrix products: 7.05 us -> 0 us
  loops' own time: 5.4 us -> 0 us
  other arithmetic: 4.9 us -> 0 us
  local copies, waits for them, and re-layouts: 10.9 us -> 8.19 us
    psum x1 -> x0, blocking collectives: 40 us -> none  [local(): grad_bias = lax.psum(bias_local, ('outer', 'inner'))]
    pallas_call x0 -> x1, Pallas kernels: none -> 27.6 us  [local(): pl.pallas_call(functools.partial(kernel, inners, outers), out_shape=(jax....]
    ppermute x30 -> x0, starting transfers between devices: 23.8 us -> none  [passed_along(): return lax.ppermute(value, axis, pairs)]
    ppermute x30 -> x0, waiting for transfers between devices: 14.8 us -> none  [passed_along(): return lax.ppermute(value, axis, pairs)]
    all_gather x1 -> x0, blocking collectives: 10.2 us -> none  [local(): seg_every = lax.all_gather(segments, 'inner', axis=1, tiled=True)]
    dot_general x30 -> x0, matrix products: 7.05 us -> none  [the longest x6 1.52 us: compute(): jnp.einsum('gtu,ud->tgd', scores_low, keys_here, preferred_element_type=j...]
    another operation x9 -> x0, loops' own time: 5.4 us -> none  [the longest x1 5.15 us: local(): lax.fori_loop(1, members, one_turn, (own_pair, (own_key, own_value), own_...]
    dynamic_slice x7 -> x0, local copies, waits for them, and re-layouts: 4.07 us -> none  [contribution(): return lax.cond(table_row[source] > 0, compute, nothing, 0)]
  transfers between devices with their start and end apart: 30 -> 0, of which waited for: 15 -> 0; matrix products, arithmetic and copies ran while one was open for 13% -> 0% of each run, Pallas kernels for 0% -> 0%
where the time goes in v1:
time: 36.9 us; the launch traced here: 36.5 us
  Pallas kernels  27.6 us (75%)
  local copies, waits for them, and re-layouts  8.19 us (22%)
  between operations  0.66 us (2%)
    pallas_call x1, Pallas kernels, local(): pl.pallas_call(functools.partial(kernel, inners, outers), out_shape=(jax....  27.6 us
    unnamed x19, local copies, waits for them, and re-layouts  8.19 us

profile of v1, /device:TPU:0, one launch (start us, length us, event | category | flops | bytes accessed | tf_op | source)
XLA Modules:
  0.0 36.5 jit_solution(7286922388471013026)
XLA Ops:
  0.6 0.0 copy-start.6
  0.6 0.7 %copy-done.6 = f32[1,7,128]{2,0,1:T(1,128)S(1)} copy-done((f32[1,7,128]{2,0,1:T(1,128)S(1)}, f32[1,7,128]{2,0,1:T(1,128)}, u32[]{:S(2)}) %copy-start.6) | copy-done | bytes 3608
  1.3 0.0 copy-start.5
  1.3 0.7 %copy-done.5 = s32[1,128]{1,0:T(1,128)S(1)} copy-done((s32[1,128]{1,0:T(1,128)S(1)}, s32[1,128]{1,0:T(1,128)}, u32[]{:S(2)}) %copy-start.5) | copy-done | bytes 536
  2.0 0.0 copy-start
  2.0 0.9 %copy-done = bf16[1,128,896]{2,1,0:T(8,128)(2,1)S(1)} copy-done((bf16[1,128,896]{2,1,0:T(8,128)(2,1)S(1)}, bf16[1,128,896]{2,1,0:T(8,128)(2,1)}, u32[]{:S(2)}) %copy-start) | copy-done | bytes 229400
  2.9 0.0 copy-start.1
  2.9 0.9 %copy-done.1 = bf16[1,128,896]{2,1,0:T(8,128)(2,1)S(1)} copy-done((bf16[1,128,896]{2,1,0:T(8,128)(2,1)S(1)}, bf16[1,128,896]{2,1,0:T(8,128)(2,1)}, u32[]{:S(2)}) %copy-start.1) | copy-done | bytes 229400
  3.9 0.0 copy-start.2
  3.9 0.9 %copy-done.2 = bf16[1,128,896]{2,1,0:T(8,128)(2,1)S(1)} copy-done((bf16[1,128,896]{2,1,0:T(8,128)(2,1)S(1)}, bf16[1,128,896]{2,1,0:T(8,128)(2,1)}, u32[]{:S(2)}) %copy-start.2) | copy-done | bytes 229400
  4.8 0.0 copy-start.3
  4.8 0.8 %copy-done.3 = bf16[1,128,128]{2,1,0:T(8,128)(2,1)S(1)} copy-done((bf16[1,128,128]{2,1,0:T(8,128)(2,1)S(1)}, bf16[1,128,128]{2,1,0:T(8,128)(2,1)}, u32[]{:S(2)}) %copy-start.3) | copy-done | bytes 32792
  5.5 0.0 copy-start.4
  5.6 0.8 %copy-done.4 = bf16[1,128,128]{2,1,0:T(8,128)(2,1)S(1)} copy-done((bf16[1,128,128]{2,1,0:T(8,128)(2,1)S(1)}, bf16[1,128,128]{2,1,0:T(8,128)(2,1)}, u32[]{:S(2)}) %copy-start.4) | copy-done | bytes 32792
  6.3 27.6 %attention_backward.1 = (bf16[128,896]{1,0:T(8,128)(2,1)S(1)}, bf16[128,128]{1,0:T(8,128)(2,1)S(1)}, bf16[128,128]{1,0:T(8,128)(2,1)S(1)}, f32[36,128]{1,0:T(8,128)S(1)}) custom-call(bf16[128,896]{1,0:T(8,128)(2,1)S(1)} %bitcast.13, bf16[128,128]{1,0:T(8,128)(2,1)S(1)} %bitcast.18, bf16[128,128]{1,0:T(8,128)(2,1)S(1)} %bitcast.19, ...), custom_call_target="tpu_custom_call" | custom-call | tf_op jit(solution)/shard_map/attention_backward/pallas_call | solution.py:279
  34.0 0.7 %copy.18 = bf16[1,128,896]{2,1,0:T(8,128)(2,1)} copy(bf16[1,128,896]{2,1,0:T(8,128)(2,1)S(1)} %bitcast.12) | data formatting | bytes 458752
  34.6 0.6 %copy.19 = bf16[1,128,128]{2,1,0:T(8,128)(2,1)} copy(bf16[1,128,128]{2,1,0:T(8,128)(2,1)S(1)} %bitcast.17) | data formatting | bytes 65536
  35.3 0.6 %copy.20 = bf16[1,128,128]{2,1,0:T(8,128)(2,1)} copy(bf16[1,128,128]{2,1,0:T(8,128)(2,1)S(1)} %bitcast.16) | data formatting | bytes 65536
  35.9 0.6 %copy.21 = f32[4608]{0:T(1024)} copy(f32[4608]{0:T(1024)S(1)} %bitcast.20) | data formatting | bytes 36864
  (1 shorter events, 0.0 us)
Async XLA Ops:
  0.6 0.7 %copy-start.6 = (f32[1,7,128]{2,0,1:T(1,128)S(1)}, f32[1,7,128]{2,0,1:T(1,128)}, u32[]{:S(2)}) copy-start(f32[1,7,128]{2,0,1:T(1,128)} %param.13) | copy-start | bytes 10756
  1.3 0.7 %copy-start.5 = (s32[1,128]{1,0:T(1,128)S(1)}, s32[1,128]{1,0:T(1,128)}, u32[]{:S(2)}) copy-start(s32[1,128]{1,0:T(1,128)} %seg_ref.1) | copy-start | bytes 1540
  2.0 0.9 %copy-start = (bf16[1,128,896]{2,1,0:T(8,128)(2,1)S(1)}, bf16[1,128,896]{2,1,0:T(8,128)(2,1)}, u32[]{:S(2)}) copy-start(bf16[1,128,896]{2,1,0:T(8,128)(2,1)} %param.8) | copy-start | bytes 688132
  2.9 0.9 %copy-start.1 = (bf16[1,128,896]{2,1,0:T(8,128)(2,1)S(1)}, bf16[1,128,896]{2,1,0:T(8,128)(2,1)}, u32[]{:S(2)}) copy-start(bf16[1,128,896]{2,1,0:T(8,128)(2,1)} %param.11) | copy-start | bytes 688132
  3.9 0.9 %copy-start.2 = (bf16[1,128,896]{2,1,0:T(8,128)(2,1)S(1)}, bf16[1,128,896]{2,1,0:T(8,128)(2,1)}, u32[]{:S(2)}) copy-start(bf16[1,128,896]{2,1,0:T(8,128)(2,1)} %param.12) | copy-start | bytes 688132
  4.8 0.8 %copy-start.3 = (bf16[1,128,128]{2,1,0:T(8,128)(2,1)S(1)}, bf16[1,128,128]{2,1,0:T(8,128)(2,1)}, u32[]{:S(2)}) copy-start(bf16[1,128,128]{2,1,0:T(8,128)(2,1)} %param.9) | copy-start | bytes 98308
  5.5 0.8 %copy-start.4 = (bf16[1,128,128]{2,1,0:T(8,128)(2,1)S(1)}, bf16[1,128,128]{2,1,0:T(8,128)(2,1)}, u32[]{:S(2)}) copy-start(bf16[1,128,128]{2,1,0:T(8,128)(2,1)} %param.10) | copy-start | bytes 98308

commit v2 on v1

--- a/solution.py
+++ b/solution.py
@@ -3,6 +3,7 @@
 
 import jax
 import jax.numpy as jnp
+import numpy as np
 from jax import lax
 from jax.experimental import pallas as pl
 from jax.experimental.pallas import tpu as pltpu
@@ -19,6 +20,7 @@
 MASKED = -1e30
 EXTRA = 16
 BIAS_ROWS = 16
+VMEM_LIMIT = 63 * 1024 * 1024
 MESH = pl.DeviceIdType.MESH
 F32 = jnp.float32
 BF16 = jnp.bfloat16
@@ -45,10 +47,12 @@
 
 
 def kernel(
-    inners, outers, q_ref, k_ref, v_ref, ao_ref, go_ref, norm_ref, seg_ref,
-    dq_ref, dk_ref, dv_ref, bias_ref,
+    inners, outers, k_hbm, v_hbm, seg_hbm, q_hbm, go_hbm, ao_hbm, norm_hbm, base_hbm, starts_hbm,
+    dq_hbm, dk_hbm, dv_hbm, bias_hbm,
+    k_ref, v_ref, seg_ref, q_ref, go_ref, ao_ref, norm_ref, base_ref, starts_ref, load_sem,
+    dq_ref, dk_ref, dv_ref, bias_ref, store_sem,
     kv, q_aug, go_aug, q_t, go_t, probs, grads, dq_acc, own_acc, part_out, part_in,
-    bias_own, bias_in, plane_own, plane_in,
+    sums, angles, bias_own, bias_in, plane_own, plane_in,
     kv_send, kv_recv, part_send, part_recv, bias_send, bias_recv, plane_send, plane_recv,
 ):
     tokens = k_ref.shape[0]
@@ -56,6 +60,22 @@
     me = lax.axis_index("inner")
     plane = lax.axis_index("outer")
 
+    loads = [
+        pltpu.make_async_copy(source, target, load_sem.at[i])
+        for i, (source, target) in enumerate([
+            (k_hbm, k_ref), (v_hbm, v_ref), (seg_hbm, seg_ref), (q_hbm, q_ref), (go_hbm, go_ref),
+            (ao_hbm, ao_ref), (norm_hbm, norm_ref), (base_hbm, base_ref), (starts_hbm, starts_ref),
+        ])
+    ]
+    for load in loads:
+        load.start()
+    stores = [
+        pltpu.make_async_copy(source, target, store_sem.at[i])
+        for i, (source, target) in enumerate([
+            (dq_ref, dq_hbm), (dk_ref, dk_hbm), (dv_ref, dv_hbm), (bias_ref, bias_hbm),
+        ])
+    ]
+
     def inner_id(step):
         return (plane, partner(me, step, inners))
 
@@ -68,6 +88,8 @@
     for step in range(1, outers):
         pl.semaphore_signal(barrier, inc=1, device_id=outer_id(step), device_id_type=MESH)
 
+    for load in loads[:3]:
+        load.wait()
     seg = seg_ref[...].astype(F32)
     row = lax.broadcasted_iota(jnp.int32, (EXTRA, tokens), 0)
     seg_rows = jnp.broadcast_to(seg, (EXTRA, tokens))
@@ -107,8 +129,8 @@
     for step in range(1, inners):
         kv_copy(step).start()
 
-    norms = norm_ref[...] * -ROOT
-    high, middle, low = pieces(norms)
+    for load in loads[3:]:
+        load.wait()
     row8 = lax.broadcasted_iota(jnp.int32, (8, tokens), 0)
     seg8 = jnp.broadcast_to(seg, (8, tokens))
     masks = jnp.where((row8 == 3) & (seg8 != 1.0), MASKED, 0.0)
@@ -123,9 +145,10 @@
         go_aug[here, :HEAD_DIM] = grad
         q_t[:, here] = jnp.transpose(query)
         go_t[:, here] = jnp.transpose(grad)
-        top = jnp.where(row8 == 0, high[g : g + 1], masks)
-        top = jnp.where(row8 == 1, middle[g : g + 1], top)
-        top = jnp.where(row8 == 2, low[g : g + 1], top)
+        high, middle, low = pieces(norm_ref[g] * -ROOT)
+        top = jnp.where(row8 == 0, high, masks)
+        top = jnp.where(row8 == 1, middle, top)
+        top = jnp.where(row8 == 2, low, top)
         full = jnp.concatenate([top, jnp.zeros((HEAD_DIM - 8, tokens), F32)], axis=0)
         q_aug[here, HEAD_DIM:] = jnp.transpose(full).astype(BF16)
         delta = -jnp.sum(
@@ -138,12 +161,22 @@
         go_aug[here, HEAD_DIM:] = side.astype(BF16)
 
     half = HEAD_DIM // 2
-    spot = lax.broadcasted_iota(jnp.int32, (tokens, HEAD_DIM), 0) + me * tokens
-    frequency = jnp.exp((lane % half).astype(F32) * (-2.0 * math.log(ROPE_BASE) / HEAD_DIM))
-    waves = jnp.sin(spot.astype(F32) * frequency + jnp.where(lane < half, 0.0, math.pi / 2))
-    turned = pltpu.roll(waves, half, 1)
-    cosine = jnp.where(lane < half, turned, waves)
-    sine = jnp.where(lane < half, waves, -turned)
+    for slot in range(inners):
+        angles[slot : slot + 1] = starts_ref[pl.ds(partner(me, slot, inners), 1)]
+
+    def both(table):
+        below = lax.broadcasted_iota(jnp.int32, table.shape, 1) < half
+        turned = pltpu.roll(table, half, 1)
+        return jnp.where(below, turned, table), jnp.where(below, table, -turned)
+
+    base_cos, base_sin = both(base_ref[...])
+    start_cos, start_sin = both(angles[...])
+    cosine = base_cos * start_cos[:1] - base_sin * start_sin[:1]
+    sine = base_sin * start_cos[:1] + base_cos * start_sin[:1]
+    base_t = jnp.transpose(base_ref[...])
+    sine_t, cosine_t = base_t[:half], base_t[half:]
+    sums[...] = jnp.zeros((HEAD_DIM, HEAD_DIM), F32)
+    sum_lane = lax.broadcasted_iota(jnp.int32, (HEAD_DIM, HEAD_DIM), 1)
 
     def unrotate(x):
         return x * cosine + pltpu.roll(x, half, 1) * sine
@@ -172,6 +205,19 @@
         key_part = dot(q_t[...], grads[...])
         return key_part, value_part
 
+    def count(slot, key_part, value_part):
+        upper, lower = key_part[:half], key_part[half:]
+        key_sum = jnp.concatenate(
+            [
+                jnp.sum(upper * cosine_t + lower * sine_t, axis=1, keepdims=True),
+                jnp.sum(lower * cosine_t - upper * sine_t, axis=1, keepdims=True),
+            ],
+            axis=0,
+        )
+        value_sum = jnp.sum(value_part, axis=1, keepdims=True)
+        held = jnp.where(sum_lane == slot, key_sum, sums[...])
+        sums[...] = jnp.where(sum_lane == half + slot, value_sum, held)
+
     def put(slot, key_part, value_part):
         part_out[slot, :HEAD_DIM] = key_part.astype(BF16)
         part_out[slot, HEAD_DIM:] = value_part.astype(BF16)
@@ -182,6 +228,8 @@
     own_acc[:HEAD_DIM] = key_part[:, :tokens]
     own_acc[HEAD_DIM:] = value_part[:, :tokens]
     put(1, key_part[:, tokens:], value_part[:, tokens:])
+    count(0, key_part[:, :tokens], value_part[:, :tokens])
+    count(1, key_part[:, tokens:], value_part[:, tokens:])
 
     def turn(g, carry):
         kv_copy(2 * g).wait_recv()
@@ -189,6 +237,8 @@
         key_part, value_part = compute(g, False)
         put(2 * g, key_part[:, :tokens], value_part[:, :tokens])
         put(2 * g + 1, key_part[:, tokens:], value_part[:, tokens:])
+        count(2 * g, key_part[:, :tokens], value_part[:, :tokens])
+        count(2 * g + 1, key_part[:, tokens:], value_part[:, tokens:])
         return carry
 
     groups = inners // 2
@@ -203,17 +253,13 @@
         full = unrotate(dq_acc[g * tokens : (g + 1) * tokens] * SCALE)
         dq_ref[:, g * HEAD_DIM : (g + 1) * HEAD_DIM] = full.astype(BF16)
         bias_own[g : g + 1] = jnp.sum(full, axis=0, keepdims=True)
-
-    total = own_acc[...]
-    for step in range(1, inners):
-        part_copy(step).wait_recv()
-        total = total + part_in[step].astype(F32)
-    key_full = unrotate(jnp.transpose(total[:HEAD_DIM]) * SCALE)
-    value_full = jnp.transpose(total[HEAD_DIM:])
-    dk_ref[...] = key_full.astype(BF16)
-    dv_ref[...] = value_full.astype(BF16)
-    bias_own[GROUP : GROUP + 1] = jnp.sum(key_full, axis=0, keepdims=True)
-    bias_own[GROUP + 1 : GROUP + 2] = jnp.sum(value_full, axis=0, keepdims=True)
+    stores[0].start()
+
+    sums_t = jnp.transpose(sums[...])
+    key_sums = sums_t[:inners]
+    key_sums = key_sums * start_cos + pltpu.roll(key_sums, half, 1) * start_sin
+    bias_own[GROUP : GROUP + 1] = jnp.sum(key_sums, axis=0, keepdims=True) * SCALE
+    bias_own[GROUP + 1 : GROUP + 2] = jnp.sum(sums_t[half : half + inners], axis=0, keepdims=True)
 
     def bias_copy(step, slot):
         return pltpu.make_async_remote_copy(
@@ -247,6 +293,18 @@
     for step in range(1, outers):
         plane_copy(step, plane).start()
     plane_in[plane] = summed
+
+    total = own_acc[...]
+    for step in range(1, inners):
+        part_copy(step).wait_recv()
+        total = total + part_in[step].astype(F32)
+    key_full = unrotate(jnp.transpose(total[:HEAD_DIM]) * SCALE)
+    value_full = jnp.transpose(total[HEAD_DIM:])
+    dk_ref[...] = key_full.astype(BF16)
+    dv_ref[...] = value_full.astype(BF16)
+    stores[1].start()
+    stores[2].start()
+
     for step in range(1, outers):
         plane_copy(step, partner(plane, step, outers)).wait_recv()
     for head in range(KV_HEADS):
@@ -257,6 +315,7 @@
         bias_ref[HEADS + head : HEADS + head + 1] = whole[GROUP : GROUP + 1]
         at = HEADS + KV_HEADS + head
         bias_ref[at : at + 1] = whole[GROUP + 1 : GROUP + 2]
+    stores[3].start()
 
     for step in range(1, inners):
         kv_copy(step).wait_send()
@@ -264,6 +323,26 @@
         bias_copy(step, me).wait_send()
     for step in range(1, outers):
         plane_copy(step, plane).wait_send()
+    for store in stores:
+        store.wait()
+
+
+def write(*refs):
+    sources, targets, sem = refs[:4], refs[4:8], refs[8]
+    copies = [
+        pltpu.make_async_copy(source, target, sem.at[i])
+        for i, (source, target) in enumerate(zip(sources, targets))
+    ]
+    for copy in copies:
+        copy.start()
+    for copy in copies:
+        copy.wait()
+
+
+def rotary(positions):
+    frequency = np.exp(np.arange(HEAD_DIM // 2) * (-2.0 * math.log(ROPE_BASE) / HEAD_DIM))
+    angles = np.asarray(positions)[:, None] * frequency[None, :]
+    return np.concatenate([np.sin(angles), np.cos(angles)], axis=1).astype(np.float32)
 
 
 def local(inners, outers, query_rot, key_rot, value_rows, attention_out, grad_out, log_norm,
@@ -274,19 +353,35 @@
     if segments.shape[0] > 1:
         example = lax.axis_index("outer") // KV_HEADS
         segments = lax.dynamic_slice_in_dim(segments, example, 1, 0)
-    vmem = pl.BlockSpec(memory_space=pltpu.VMEM)
+    hbm = pl.BlockSpec(memory_space=pltpu.HBM)
     sems = pltpu.SemaphoreType.DMA
+    shapes = (
+        jax.ShapeDtypeStruct((tokens, GROUP * HEAD_DIM), BF16),
+        jax.ShapeDtypeStruct((tokens, HEAD_DIM), BF16),
+        jax.ShapeDtypeStruct((tokens, HEAD_DIM), BF16),
+        jax.ShapeDtypeStruct((HEADS + 2 * KV_HEADS, HEAD_DIM), F32),
+    )
     outs = pl.pallas_call(
         functools.partial(kernel, inners, outers),
-        out_shape=(
-            jax.ShapeDtypeStruct((tokens, GROUP * HEAD_DIM), BF16),
-            jax.ShapeDtypeStruct((tokens, HEAD_DIM), BF16),
-            jax.ShapeDtypeStruct((tokens, HEAD_DIM), BF16),
-            jax.ShapeDtypeStruct((HEADS + 2 * KV_HEADS, HEAD_DIM), F32),
-        ),
-        in_specs=[vmem] * 7,
-        out_specs=(vmem,) * 4,
+        out_shape=shapes,
+        in_specs=[hbm] * 9,
+        out_specs=(hbm,) * 4,
         scratch_shapes=[
+            pltpu.VMEM((tokens, HEAD_DIM), BF16),
+            pltpu.VMEM((tokens, HEAD_DIM), BF16),
+            pltpu.VMEM((1, tokens), jnp.int32),
+            pltpu.VMEM((tokens, GROUP * HEAD_DIM), BF16),
+            pltpu.VMEM((tokens, GROUP * HEAD_DIM), BF16),
+            pltpu.VMEM((tokens, GROUP * HEAD_DIM), BF16),
+            pltpu.VMEM((GROUP, 1, tokens), F32),
+            pltpu.VMEM((tokens, HEAD_DIM), F32),
+            pltpu.VMEM((inners, HEAD_DIM), F32),
+            sems((9,)),
+            pltpu.VMEM((tokens, GROUP * HEAD_DIM), BF16),
+            pltpu.VMEM((tokens, HEAD_DIM), BF16),
+            pltpu.VMEM((tokens, HEAD_DIM), BF16),
+            pltpu.VMEM((HEADS + 2 * KV_HEADS, HEAD_DIM), F32),
+            sems((4,)),
             pltpu.VMEM((inners, 3 * HEAD_DIM, tokens), BF16),
             pltpu.VMEM((rows, 2 * HEAD_DIM), BF16),
             pltpu.VMEM((rows, 2 * HEAD_DIM), BF16),
@@ -298,6 +393,8 @@
             pltpu.VMEM((2 * HEAD_DIM, tokens), F32),
             pltpu.VMEM((inners, 2 * HEAD_DIM, tokens), BF16),
             pltpu.VMEM((inners, 2 * HEAD_DIM, tokens), BF16),
+            pltpu.VMEM((HEAD_DIM, HEAD_DIM), F32),
+            pltpu.VMEM((inners, HEAD_DIM), F32),
             pltpu.VMEM((BIAS_ROWS, HEAD_DIM), F32),
             pltpu.VMEM((inners, BIAS_ROWS, HEAD_DIM), F32),
             pltpu.VMEM((BIAS_ROWS, HEAD_DIM), F32),
@@ -306,10 +403,23 @@
             sems((inners,)), sems((inners,)), sems((outers,)), sems((outers,)),
         ],
         compiler_params=pltpu.CompilerParams(
-            collective_id=0, has_side_effects=True, vmem_limit_bytes=48 * 1024 * 1024
+            collective_id=0, has_side_effects=True, vmem_limit_bytes=VMEM_LIMIT
         ),
         name="attention_backward",
-    )(query_rot[0], key_rot[0], value_rows[0], attention_out[0], grad_out[0], log_norm[0], segments)
+    )(
+        key_rot[0], value_rows[0], segments, query_rot[0], grad_out[0], attention_out[0],
+        log_norm.reshape(GROUP, 1, tokens), jnp.asarray(rotary(np.arange(tokens))),
+        jnp.asarray(rotary(np.arange(inners) * tokens)),
+    )
+    outs = pl.pallas_call(
+        write,
+        out_shape=shapes,
+        in_specs=[hbm] * 4,
+        out_specs=(hbm,) * 4,
+        scratch_shapes=[sems((4,))],
+        compiler_params=pltpu.CompilerParams(vmem_limit_bytes=VMEM_LIMIT),
+        name="write_results",
+    )(*outs)
     return outs[0][None], outs[1][None], outs[2][None], outs[3].reshape(-1)
 
 

time: 36.9 us -> 37.6 us (1.019)
  Pallas kernels: 27.6 us -> 36.8 us
  local copies, waits for them, and re-layouts: 8.19 us -> 0 us
    pallas_call x1 -> x2, Pallas kernels: 27.6 us -> 36.8 us  [the longest x1 26.2 us: local(): pl.pallas_call(functools.partial(kernel, inners, outers), out_shape=shape...]
    unnamed x19 -> x0, local copies, waits for them, and re-layouts: 8.19 us -> none
where the time goes in v2:
time: 37.6 us; the launch traced here: 37.5 us
  Pallas kernels  36.8 us (98%)
  between operations  0.64 us (2%)
    pallas_call x1, Pallas kernels, local(): pl.pallas_call(functools.partial(kernel, inners, outers), out_shape=shape...  26.2 us
    pallas_call x1, Pallas kernels, local(): pl.pallas_call(write, out_shape=shapes, in_specs=[hbm] * 4, out_specs=(hb...  10.6 us

profile of v2, /device:TPU:0, one launch (start us, length us, event | category | flops | bytes accessed | tf_op | source)
XLA Modules:
  0.0 37.5 jit_solution(566508286060754169)
XLA Ops:
  0.6 26.2 %attention_backward.1 = (bf16[128,896]{1,0:T(8,128)(2,1)}, bf16[128,128]{1,0:T(8,128)(2,1)}, bf16[128,128]{1,0:T(8,128)(2,1)}, f32[36,128]{1,0:T(8,128)}) custom-call(bf16[128,128]{1,0:T(8,128)(2,1)} %bitcast.13, bf16[128,128]{1,0:T(8,128)(2,1)} %bitcast.14, s32[1,128]{1,0:T(1,128)} %seg_hbm.1, bf16[128,896]{1,0:T(8,128)(2,1)} %bitcast.10, ...), custom_call_target="tpu_custom_call" | custom-call | tf_op jit(solution)/shard_map/attention_backward/pallas_call | solution.py:364
  26.8 10.6 %write_results.1 = (bf16[128,896]{1,0:T(8,128)(2,1)}, bf16[128,128]{1,0:T(8,128)(2,1)}, bf16[128,128]{1,0:T(8,128)(2,1)}, f32[36,128]{1,0:T(8,128)}) custom-call(bf16[128,896]{1,0:T(8,128)(2,1)} %get-tuple-element.12.refs_0_, bf16[128,128]{1,0:T(8,128)(2,1)} %get-tuple-element.13.refs_1_, bf16[128,128]{1,0:T(8,128)(2,1)} %get-tuple-element.14.refs_2_, ...), custom_call_target="tpu_custom_call" | custom-call | tf_op jit(solution)/shard_map/write_results/pallas_call | solution.py:414

commit v3 on v2

--- a/solution.py
+++ b/solution.py
@@ -51,9 +51,10 @@
     dq_hbm, dk_hbm, dv_hbm, bias_hbm,
     k_ref, v_ref, seg_ref, q_ref, go_ref, ao_ref, norm_ref, base_ref, starts_ref, load_sem,
     dq_ref, dk_ref, dv_ref, bias_ref, store_sem,
-    kv, q_aug, go_aug, q_t, go_t, probs, grads, dq_acc, own_acc, part_out, part_in,
+    kv, q_aug, go_aug, q_t, go_t, probs, grads, dq_acc, own_acc, kept, pair_out, pair_in,
+    part_out, part_in,
     sums, angles, bias_own, bias_in, plane_own, plane_in,
-    kv_send, kv_recv, part_send, part_recv, bias_send, bias_recv, plane_send, plane_recv,
+    kv_send, kv_recv, pair_send, pair_recv, part_send, part_recv, bias_send, bias_recv, plane_send, plane_recv,
 ):
     tokens = k_ref.shape[0]
     rows = GROUP * tokens
@@ -116,6 +117,26 @@
             device_id_type=MESH,
         )
 
+    def forward(step):
+        return pltpu.make_async_remote_copy(
+            src_ref=kv.at[step, pl.ds(0, sent)],
+            dst_ref=kv.at[step + 1, pl.ds(0, sent)],
+            send_sem=kv_send.at[step + 1],
+            recv_sem=kv_recv.at[step + 1],
+            device_id=inner_id(1),
+            device_id_type=MESH,
+        )
+
+    def pair_copy(g):
+        return pltpu.make_async_remote_copy(
+            src_ref=pair_out.at[g],
+            dst_ref=pair_in.at[g],
+            send_sem=pair_send.at[g],
+            recv_sem=pair_recv.at[g],
+            device_id=inner_id(1),
+            device_id_type=MESH,
+        )
+
     def part_copy(step):
         return pltpu.make_async_remote_copy(
             src_ref=part_out.at[step],
@@ -126,7 +147,10 @@
             device_id_type=MESH,
         )
 
-    for step in range(1, inners):
+    groups = inners // 2
+    order = [1, 3, 2] if groups == 4 else list(range(1, groups))
+    direct = [1] + [2 * g for g in range(1, groups)]
+    for step in direct:
         kv_copy(step).start()
 
     for load in loads[3:]:
@@ -218,35 +242,53 @@
         held = jnp.where(sum_lane == slot, key_sum, sums[...])
         sums[...] = jnp.where(sum_lane == half + slot, value_sum, held)
 
-    def put(slot, key_part, value_part):
-        part_out[slot, :HEAD_DIM] = key_part.astype(BF16)
-        part_out[slot, HEAD_DIM:] = value_part.astype(BF16)
-        part_copy(slot).start()
+    def pass_on(g):
+        kv_copy(2 * g).wait_recv()
+        forward(2 * g).start()
+
+    def turn(g):
+        forward(2 * g).wait_recv()
+        key_part, value_part = compute(g, False)
+        pair_out[g, :HEAD_DIM] = key_part[:, tokens:].astype(BF16)
+        pair_out[g, HEAD_DIM:] = value_part[:, tokens:].astype(BF16)
+        pair_copy(g).start()
+        kept[g, :HEAD_DIM] = key_part[:, :tokens]
+        kept[g, HEAD_DIM:] = value_part[:, :tokens]
+        count(2 * g, key_part[:, :tokens], value_part[:, :tokens])
+        count(2 * g + 1, key_part[:, tokens:], value_part[:, tokens:])
+
+    def send_home(g):
+        pair_copy(g).wait_recv()
+        part_out[2 * g] = (kept[g] + pair_in[g].astype(F32)).astype(BF16)
+        part_copy(2 * g).start()
 
     kv_copy(1).wait_recv()
     key_part, value_part = compute(0, True)
+    part_out[1, :HEAD_DIM] = key_part[:, tokens:].astype(BF16)
+    part_out[1, HEAD_DIM:] = value_part[:, tokens:].astype(BF16)
+    part_copy(1).start()
     own_acc[:HEAD_DIM] = key_part[:, :tokens]
     own_acc[HEAD_DIM:] = value_part[:, :tokens]
-    put(1, key_part[:, tokens:], value_part[:, tokens:])
     count(0, key_part[:, :tokens], value_part[:, :tokens])
     count(1, key_part[:, tokens:], value_part[:, tokens:])
-
-    def turn(g, carry):
-        kv_copy(2 * g).wait_recv()
-        kv_copy(2 * g + 1).wait_recv()
-        key_part, value_part = compute(g, False)
-        put(2 * g, key_part[:, :tokens], value_part[:, :tokens])
-        put(2 * g + 1, key_part[:, tokens:], value_part[:, tokens:])
-        count(2 * g, key_part[:, :tokens], value_part[:, :tokens])
-        count(2 * g + 1, key_part[:, tokens:], value_part[:, tokens:])
-        return carry
-
-    groups = inners // 2
     if groups <= 4:
-        for g in range(1, groups):
-            turn(g, 0)
+        for i, g in enumerate(order):
+            if i == 0:
+                pass_on(g)
+            if i + 1 < len(order):
+                pass_on(order[i + 1])
+            turn(g)
+            if i > 0:
+                send_home(order[i - 1])
     else:
-        lax.fori_loop(1, groups, turn, 0)
+
+        def whole_turn(g, carry):
+            pass_on(g)
+            turn(g)
+            send_home(g)
+            return carry
+
+        lax.fori_loop(1, groups, whole_turn, 0)
 
     bias_own[...] = jnp.zeros((BIAS_ROWS, HEAD_DIM), F32)
     for g in range(GROUP):
@@ -255,6 +297,8 @@
         bias_own[g : g + 1] = jnp.sum(full, axis=0, keepdims=True)
     stores[0].start()
 
+    if groups <= 4:
+        send_home(order[-1])
     sums_t = jnp.transpose(sums[...])
     key_sums = sums_t[:inners]
     key_sums = key_sums * start_cos + pltpu.roll(key_sums, half, 1) * start_sin
@@ -295,7 +339,7 @@
     plane_in[plane] = summed
 
     total = own_acc[...]
-    for step in range(1, inners):
+    for step in direct:
         part_copy(step).wait_recv()
         total = total + part_in[step].astype(F32)
     key_full = unrotate(jnp.transpose(total[:HEAD_DIM]) * SCALE)
@@ -317,9 +361,13 @@
         bias_ref[at : at + 1] = whole[GROUP + 1 : GROUP + 2]
     stores[3].start()
 
-    for step in range(1, inners):
+    for step in direct:
         kv_copy(step).wait_send()
         part_copy(step).wait_send()
+    for g in range(1, groups):
+        forward(2 * g).wait_send()
+        pair_copy(g).wait_send()
+    for step in range(1, inners):
         bias_copy(step, me).wait_send()
     for step in range(1, outers):
         plane_copy(step, plane).wait_send()
@@ -328,15 +376,16 @@
 
 
 def write(*refs):
-    sources, targets, sem = refs[:4], refs[4:8], refs[8]
-    copies = [
-        pltpu.make_async_copy(source, target, sem.at[i])
-        for i, (source, target) in enumerate(zip(sources, targets))
-    ]
-    for copy in copies:
-        copy.start()
-    for copy in copies:
-        copy.wait()
+    sources, targets, held, sem = refs[:4], refs[4:8], refs[8:12], refs[12]
+    loads = [pltpu.make_async_copy(sources[i], held[i], sem.at[i]) for i in range(4)]
+    stores = [pltpu.make_async_copy(held[i], targets[i], sem.at[4 + i]) for i in range(4)]
+    for load in loads:
+        load.start()
+    for load, store in zip(loads, stores):
+        load.wait()
+        store.start()
+    for store in stores:
+        store.wait()
 
 
 def rotary(positions):
@@ -391,6 +440,9 @@
             pltpu.VMEM((rows, 2 * tokens), BF16),
             pltpu.VMEM((rows, HEAD_DIM), F32),
             pltpu.VMEM((2 * HEAD_DIM, tokens), F32),
+            pltpu.VMEM((inners // 2, 2 * HEAD_DIM, tokens), F32),
+            pltpu.VMEM((inners // 2, 2 * HEAD_DIM, tokens), BF16),
+            pltpu.VMEM((inners // 2, 2 * HEAD_DIM, tokens), BF16),
             pltpu.VMEM((inners, 2 * HEAD_DIM, tokens), BF16),
             pltpu.VMEM((inners, 2 * HEAD_DIM, tokens), BF16),
             pltpu.VMEM((HEAD_DIM, HEAD_DIM), F32),
@@ -399,7 +451,8 @@
             pltpu.VMEM((inners, BIAS_ROWS, HEAD_DIM), F32),
             pltpu.VMEM((BIAS_ROWS, HEAD_DIM), F32),
             pltpu.VMEM((outers, BIAS_ROWS, HEAD_DIM), F32),
-            sems((inners,)), sems((inners,)), sems((inners,)), sems((inners,)),
+            sems((inners,)), sems((inners,)), sems((inners // 2,)), sems((inners // 2,)),
+            sems((inners,)), sems((inners,)),
             sems((inners,)), sems((inners,)), sems((outers,)), sems((outers,)),
         ],
         compiler_params=pltpu.CompilerParams(
@@ -416,7 +469,7 @@
         out_shape=shapes,
         in_specs=[hbm] * 4,
         out_specs=(hbm,) * 4,
-        scratch_shapes=[sems((4,))],
+        scratch_shapes=[pltpu.VMEM(shape.shape, shape.dtype) for shape in shapes] + [sems((8,))],
         compiler_params=pltpu.CompilerParams(vmem_limit_bytes=VMEM_LIMIT),
         name="write_results",
     )(*outs)

time: 37.6 us -> 27.9 us (0.74)
  Pallas kernels: 36.8 us -> 27.1 us
    pallas_call x1, Pallas kernels: 10.6 us -> 1.71 us  [local(): pl.pallas_call(write, out_shape=shapes, in_specs=[hbm] * 4, out_specs=(hb...]
    pallas_call x1, Pallas kernels: 26.2 us -> 25.4 us  [local(): pl.pallas_call(functools.partial(kernel, inners, outers), out_shape=shape...]
where the time goes in v3:
time: 27.9 us; the launch traced here: 27.7 us
  Pallas kernels  27.1 us (97%)
  between operations  0.64 us (2%)
    pallas_call x1, Pallas kernels, local(): pl.pallas_call(functools.partial(kernel, inners, outers), out_shape=shape...  25.4 us
    pallas_call x1, Pallas kernels, local(): pl.pallas_call(write, out_shape=shapes, in_specs=[hbm] * 4, out_specs=(hb...  1.71 us

profile of v3, /device:TPU:0, one launch (start us, length us, event | category | flops | bytes accessed | tf_op | source)
XLA Modules:
  0.0 27.7 jit_solution(17284124681762034931)
XLA Ops:
  0.6 25.4 %attention_backward.1 = (bf16[128,896]{1,0:T(8,128)(2,1)}, bf16[128,128]{1,0:T(8,128)(2,1)}, bf16[128,128]{1,0:T(8,128)(2,1)}, f32[36,128]{1,0:T(8,128)}) custom-call(bf16[128,128]{1,0:T(8,128)(2,1)} %bitcast.13, bf16[128,128]{1,0:T(8,128)(2,1)} %bitcast.14, s32[1,128]{1,0:T(1,128)} %seg_hbm.1, bf16[128,896]{1,0:T(8,128)(2,1)} %bitcast.10, ...), custom_call_target="tpu_custom_call" | custom-call | tf_op jit(solution)/shard_map/attention_backward/pallas_call | solution.py:413
  26.0 1.7 %write_results.1 = (bf16[128,896]{1,0:T(8,128)(2,1)}, bf16[128,128]{1,0:T(8,128)(2,1)}, bf16[128,128]{1,0:T(8,128)(2,1)}, f32[36,128]{1,0:T(8,128)}) custom-call(bf16[128,896]{1,0:T(8,128)(2,1)} %get-tuple-element.12.refs_0_, bf16[128,128]{1,0:T(8,128)(2,1)} %get-tuple-element.13.refs_1_, bf16[128,128]{1,0:T(8,128)(2,1)} %get-tuple-element.14.refs_2_, ...), custom_call_target="tpu_custom_call" | custom-call | tf_op jit(solution)/shard_map/write_results/pallas_call | solution.py:467

commit v4 on v3

--- a/solution.py
+++ b/solution.py
@@ -16,7 +16,6 @@
 ROPE_BASE = 1000000.0
 ROOT = math.sqrt(HEAD_DIM)
 SCALE = 1.0 / ROOT
-EXP2_SCALE = math.log2(math.e) / ROOT
 MASKED = -1e30
 EXTRA = 16
 BIAS_ROWS = 16
@@ -205,7 +204,7 @@
     def unrotate(x):
         return x * cosine + pltpu.roll(x, half, 1) * sine
 
-    chunk = 256
+    chunk = rows if tokens <= 128 else 256
     starts = list(range(0, rows, chunk))
 
     def compute(g, first):
@@ -216,7 +215,7 @@
         for start in starts:
             here = slice(start, min(start + chunk, rows))
             scores = dot(q_aug[here], keys_t)
-            chances = jnp.exp2(scores * EXP2_SCALE)
+            chances = jnp.exp(scores * SCALE)
             probs[here] = chances.astype(BF16)
             low_grads = (chances * dot(go_aug[here], values_t)).astype(BF16)
             grads[here] = low_grads

time: 27.9 us -> 27.3 us (0.978)
  Pallas kernels: 27.1 us -> 26.5 us
    pallas_call x1, Pallas kernels: 25.4 us -> 24.8 us  [local(): pl.pallas_call(functools.partial(kernel, inners, outers), out_shape=shape...]
where the time goes in v4:
time: 27.3 us; the launch traced here: 27.1 us
  Pallas kernels  26.5 us (97%)
  between operations  0.64 us (2%)
    pallas_call x1, Pallas kernels, local(): pl.pallas_call(functools.partial(kernel, inners, outers), out_shape=shape...  24.8 us
    pallas_call x1, Pallas kernels, local(): pl.pallas_call(write, out_shape=shapes, in_specs=[hbm] * 4, out_specs=(hb...  1.71 us

profile of v4, /device:TPU:0, one launch (start us, length us, event | category | flops | bytes accessed | tf_op | source)
XLA Modules:
  0.0 27.1 jit_solution(9452229449594650397)
XLA Ops:
  0.6 24.8 %attention_backward.1 = (bf16[128,896]{1,0:T(8,128)(2,1)}, bf16[128,128]{1,0:T(8,128)(2,1)}, bf16[128,128]{1,0:T(8,128)(2,1)}, f32[36,128]{1,0:T(8,128)}) custom-call(bf16[128,128]{1,0:T(8,128)(2,1)} %bitcast.13, bf16[128,128]{1,0:T(8,128)(2,1)} %bitcast.14, s32[1,128]{1,0:T(1,128)} %seg_hbm.1, bf16[128,896]{1,0:T(8,128)(2,1)} %bitcast.10, ...), custom_call_target="tpu_custom_call" | custom-call | tf_op jit(solution)/shard_map/attention_backward/pallas_call | solution.py:412
  25.4 1.7 %write_results.1 = (bf16[128,896]{1,0:T(8,128)(2,1)}, bf16[128,128]{1,0:T(8,128)(2,1)}, bf16[128,128]{1,0:T(8,128)(2,1)}, f32[36,128]{1,0:T(8,128)}) custom-call(bf16[128,896]{1,0:T(8,128)(2,1)} %get-tuple-element.12.refs_0_, bf16[128,128]{1,0:T(8,128)(2,1)} %get-tuple-element.13.refs_1_, bf16[128,128]{1,0:T(8,128)(2,1)} %get-tuple-element.14.refs_2_, ...), custom_call_target="tpu_custom_call" | custom-call | tf_op jit(solution)/shard_map/write_results/pallas_call | solution.py:466

commit v5 on v4

--- a/solution.py
+++ b/solution.py
@@ -52,7 +52,7 @@
     dq_ref, dk_ref, dv_ref, bias_ref, store_sem,
     kv, q_aug, go_aug, q_t, go_t, probs, grads, dq_acc, own_acc, kept, pair_out, pair_in,
     part_out, part_in,
-    sums, angles, bias_own, bias_in, plane_own, plane_in,
+    sums, angles, bias_own, bias_in, plane_in,
     kv_send, kv_recv, pair_send, pair_recv, part_send, part_recv, bias_send, bias_recv, plane_send, plane_recv,
 ):
     tokens = k_ref.shape[0]
@@ -79,14 +79,25 @@
     def inner_id(step):
         return (plane, partner(me, step, inners))
 
-    def outer_id(step):
-        return (partner(plane, step, outers), me)
+    def beside(way):
+        return (plane + way, me)
+
+    has_left = plane > 0
+    has_right = plane < outers - 1
+    neighbours = (plane + outers - 1) // outers + (2 * outers - 2 - plane) // outers
 
     barrier = pltpu.get_barrier_semaphore()
     for step in range(1, inners):
         pl.semaphore_signal(barrier, inc=1, device_id=inner_id(step), device_id_type=MESH)
-    for step in range(1, outers):
-        pl.semaphore_signal(barrier, inc=1, device_id=outer_id(step), device_id_type=MESH)
+
+    @pl.when(has_left)
+    def _():
+        pl.semaphore_signal(barrier, inc=1, device_id=beside(-1), device_id_type=MESH)
+
+    @pl.when(has_right)
+    def _():
+        pl.semaphore_signal(barrier, inc=1, device_id=beside(1), device_id_type=MESH)
+
 
     for load in loads[:3]:
         load.wait()
@@ -102,7 +113,7 @@
     for slot in range(inners):
         kv[slot, 2 * HEAD_DIM + EXTRA :] = jnp.zeros((HEAD_DIM - EXTRA, tokens), BF16)
 
-    pl.semaphore_wait(barrier, inners + outers - 2)
+    pl.semaphore_wait(barrier, inners - 1 + neighbours)
 
     sent = 2 * HEAD_DIM + EXTRA
 
@@ -296,8 +307,6 @@
         bias_own[g : g + 1] = jnp.sum(full, axis=0, keepdims=True)
     stores[0].start()
 
-    if groups <= 4:
-        send_home(order[-1])
     sums_t = jnp.transpose(sums[...])
     key_sums = sums_t[:inners]
     key_sums = key_sums * start_cos + pltpu.roll(key_sums, half, 1) * start_sin
@@ -314,28 +323,49 @@
             device_id_type=MESH,
         )
 
-    def plane_copy(step, slot):
-        return pltpu.make_async_remote_copy(
-            src_ref=plane_own,
+    def rightward(far, slot):
+        return pltpu.make_async_remote_copy(
+            src_ref=plane_in.at[slot],
             dst_ref=plane_in.at[slot],
-            send_sem=plane_send.at[step],
-            recv_sem=plane_recv.at[step],
-            device_id=outer_id(step),
-            device_id_type=MESH,
-        )
+            send_sem=plane_send.at[far],
+            recv_sem=plane_recv.at[far],
+            device_id=beside(1),
+            device_id_type=MESH,
+        )
+
+    def leftward(far, slot):
+        return pltpu.make_async_remote_copy(
+            src_ref=plane_in.at[slot],
+            dst_ref=plane_in.at[slot],
+            send_sem=plane_send.at[outers + far],
+            recv_sem=plane_recv.at[outers + far],
+            device_id=beside(-1),
+            device_id_type=MESH,
+        )
+
+    def send_right(far, act):
+        @pl.when((plane - far + 1 >= 0) & has_right)
+        def _():
+            act(rightward(far, plane - far + 1))
+
+    def send_left(far, act):
+        @pl.when((plane + far - 1 < outers) & has_left)
+        def _():
+            act(leftward(far, plane + far - 1))
 
     for step in range(1, inners):
         bias_copy(step, me).start()
+    if groups <= 4:
+        send_home(order[-1])
     bias_in[me] = bias_own[...]
     for step in range(1, inners):
         bias_copy(step, partner(me, step, inners)).wait_recv()
     summed = bias_in[0]
     for slot in range(1, inners):
         summed = summed + bias_in[slot]
-    plane_own[...] = summed
-    for step in range(1, outers):
-        plane_copy(step, plane).start()
     plane_in[plane] = summed
+    send_right(1, lambda copy: copy.start())
+    send_left(1, lambda copy: copy.start())
 
     total = own_acc[...]
     for step in direct:
@@ -348,8 +378,21 @@
     stores[1].start()
     stores[2].start()
 
-    for step in range(1, outers):
-        plane_copy(step, partner(plane, step, outers)).wait_recv()
+    for far in range(1, outers):
+
+        @pl.when(plane - far >= 0)
+        def _(far=far):
+            rightward(far, plane - far).wait_recv()
+
+        if far + 1 < outers:
+            send_right(far + 1, lambda copy: copy.start())
+
+        @pl.when(plane + far < outers)
+        def _(far=far):
+            leftward(far, plane + far).wait_recv()
+
+        if far + 1 < outers:
+            send_left(far + 1, lambda copy: copy.start())
     for head in range(KV_HEADS):
         whole = plane_in[head]
         for other in range(head + KV_HEADS, outers, KV_HEADS):
@@ -368,8 +411,9 @@
         pair_copy(g).wait_send()
     for step in range(1, inners):
         bias_copy(step, me).wait_send()
-    for step in range(1, outers):
-        plane_copy(step, plane).wait_send()
+    for far in range(1, outers):
+        send_right(far, lambda copy: copy.wait_send())
+        send_left(far, lambda copy: copy.wait_send())
     for store in stores:
         store.wait()
 
@@ -448,11 +492,10 @@
             pltpu.VMEM((inners, HEAD_DIM), F32),
             pltpu.VMEM((BIAS_ROWS, HEAD_DIM), F32),
             pltpu.VMEM((inners, BIAS_ROWS, HEAD_DIM), F32),
-            pltpu.VMEM((BIAS_ROWS, HEAD_DIM), F32),
             pltpu.VMEM((outers, BIAS_ROWS, HEAD_DIM), F32),
             sems((inners,)), sems((inners,)), sems((inners // 2,)), sems((inners // 2,)),
             sems((inners,)), sems((inners,)),
-            sems((inners,)), sems((inners,)), sems((outers,)), sems((outers,)),
+            sems((inners,)), sems((inners,)), sems((2 * outers,)), sems((2 * outers,)),
         ],
         compiler_params=pltpu.CompilerParams(
             collective_id=0, has_side_effects=True, vmem_limit_bytes=VMEM_LIMIT

time: 27.3 us -> 30.8 us (1.13)
  Pallas kernels: 26.5 us -> 30 us
    pallas_call x1, Pallas kernels: 24.8 us -> 28.3 us  [local(): pl.pallas_call(functools.partial(kernel, inners, outers), out_shape=shape...]
where the time goes in v5:
time: 30.8 us; the launch traced here: 30.7 us
  Pallas kernels  30 us (97%)
  between operations  0.64 us (2%)
    pallas_call x1, Pallas kernels, local(): pl.pallas_call(functools.partial(kernel, inners, outers), out_shape=shape...  28.3 us
    pallas_call x1, Pallas kernels, local(): pl.pallas_call(write, out_shape=shapes, in_specs=[hbm] * 4, out_specs=(hb...  1.71 us

profile of v5, /device:TPU:0, one launch (start us, length us, event | category | flops | bytes accessed | tf_op | source)
XLA Modules:
  0.0 30.7 jit_solution(13979752165978762164)
XLA Ops:
  0.6 28.3 %attention_backward.1 = (bf16[128,896]{1,0:T(8,128)(2,1)}, bf16[128,128]{1,0:T(8,128)(2,1)}, bf16[128,128]{1,0:T(8,128)(2,1)}, f32[36,128]{1,0:T(8,128)}) custom-call(bf16[128,128]{1,0:T(8,128)(2,1)} %bitcast.13, bf16[128,128]{1,0:T(8,128)(2,1)} %bitcast.14, s32[1,128]{1,0:T(1,128)} %seg_hbm.1, bf16[128,896]{1,0:T(8,128)(2,1)} %bitcast.10, ...), custom_call_target="tpu_custom_call" | custom-call | tf_op jit(solution)/shard_map/attention_backward/pallas_call | solution.py:456
  28.9 1.7 %write_results.1 = (bf16[128,896]{1,0:T(8,128)(2,1)}, bf16[128,128]{1,0:T(8,128)(2,1)}, bf16[128,128]{1,0:T(8,128)(2,1)}, f32[36,128]{1,0:T(8,128)}) custom-call(bf16[128,896]{1,0:T(8,128)(2,1)} %get-tuple-element.12.refs_0_, bf16[128,128]{1,0:T(8,128)(2,1)} %get-tuple-element.13.refs_1_, bf16[128,128]{1,0:T(8,128)(2,1)} %get-tuple-element.14.refs_2_, ...), custom_call_target="tpu_custom_call" | custom-call | tf_op jit(solution)/shard_map/write_results/pallas_call | solution.py:509

commit v6 on v4

--- a/solution.py
+++ b/solution.py
@@ -52,7 +52,7 @@
     dq_ref, dk_ref, dv_ref, bias_ref, store_sem,
     kv, q_aug, go_aug, q_t, go_t, probs, grads, dq_acc, own_acc, kept, pair_out, pair_in,
     part_out, part_in,
-    sums, angles, bias_own, bias_in, plane_own, plane_in,
+    prob_sums, angles, bias_own, bias_in, plane_own, plane_in,
     kv_send, kv_recv, pair_send, pair_recv, part_send, part_recv, bias_send, bias_recv, plane_send, plane_recv,
 ):
     tokens = k_ref.shape[0]
@@ -147,7 +147,6 @@
         )
 
     groups = inners // 2
-    order = [1, 3, 2] if groups == 4 else list(range(1, groups))
     direct = [1] + [2 * g for g in range(1, groups)]
     for step in direct:
         kv_copy(step).start()
@@ -196,10 +195,11 @@
     start_cos, start_sin = both(angles[...])
     cosine = base_cos * start_cos[:1] - base_sin * start_sin[:1]
     sine = base_sin * start_cos[:1] + base_cos * start_sin[:1]
-    base_t = jnp.transpose(base_ref[...])
-    sine_t, cosine_t = base_t[:half], base_t[half:]
-    sums[...] = jnp.zeros((HEAD_DIM, HEAD_DIM), F32)
-    sum_lane = lax.broadcasted_iota(jnp.int32, (HEAD_DIM, HEAD_DIM), 1)
+    base_turned = pltpu.roll(base_ref[...], half, 1)
+
+    def waves(slot):
+        start_cos, start_sin = both(angles[pl.ds(slot, 1)])
+        return (base_ref[...] * start_cos + base_turned * start_sin).astype(BF16)
 
     def unrotate(x):
         return x * cosine + pltpu.roll(x, half, 1) * sine
@@ -207,39 +207,31 @@
     chunk = rows if tokens <= 128 else 256
     starts = list(range(0, rows, chunk))
 
-    def compute(g, first):
+    def query_side(g, first):
         block = jnp.concatenate([kv[2 * g], kv[2 * g + 1]], axis=1)
         values_t = jnp.concatenate([block[:HEAD_DIM], block[2 * HEAD_DIM :]], axis=0)
         keys_t = block[HEAD_DIM:]
-        keys = jnp.transpose(block[HEAD_DIM : 2 * HEAD_DIM])
+        turns = jnp.concatenate([waves(2 * g), waves(2 * g + 1)], axis=0)
+        keys = jnp.concatenate([jnp.transpose(block[HEAD_DIM : 2 * HEAD_DIM]), turns], axis=1)
         for start in starts:
             here = slice(start, min(start + chunk, rows))
-            scores = dot(q_aug[here], keys_t)
-            chances = jnp.exp(scores * SCALE)
-            probs[here] = chances.astype(BF16)
+            chances = jnp.exp(dot(q_aug[here], keys_t) * SCALE)
+            probs[g, here] = chances.astype(BF16)
             low_grads = (chances * dot(go_aug[here], values_t)).astype(BF16)
-            grads[here] = low_grads
+            grads[g, here] = low_grads
             part = dot(low_grads, keys)
+            chance_part = chances[:, :HEAD_DIM]
+            for col in range(HEAD_DIM, 2 * tokens, HEAD_DIM):
+                chance_part = chance_part + chances[:, col : col + HEAD_DIM]
             if first:
                 dq_acc[here] = part
+                prob_sums[here] = chance_part
             else:
                 dq_acc[here] += part
-        value_part = dot(go_t[...], probs[...])
-        key_part = dot(q_t[...], grads[...])
-        return key_part, value_part
-
-    def count(slot, key_part, value_part):
-        upper, lower = key_part[:half], key_part[half:]
-        key_sum = jnp.concatenate(
-            [
-                jnp.sum(upper * cosine_t + lower * sine_t, axis=1, keepdims=True),
-                jnp.sum(lower * cosine_t - upper * sine_t, axis=1, keepdims=True),
-            ],
-            axis=0,
-        )
-        value_sum = jnp.sum(value_part, axis=1, keepdims=True)
-        held = jnp.where(sum_lane == slot, key_sum, sums[...])
-        sums[...] = jnp.where(sum_lane == half + slot, value_sum, held)
+                prob_sums[here] += chance_part
+
+    def key_side(g):
+        return dot(q_t[...], grads[g]), dot(go_t[...], probs[g])
 
     def pass_on(g):
         kv_copy(2 * g).wait_recv()
@@ -247,14 +239,15 @@
 
     def turn(g):
         forward(2 * g).wait_recv()
-        key_part, value_part = compute(g, False)
+        query_side(g, False)
+
+    def give(g):
+        key_part, value_part = key_side(g)
         pair_out[g, :HEAD_DIM] = key_part[:, tokens:].astype(BF16)
         pair_out[g, HEAD_DIM:] = value_part[:, tokens:].astype(BF16)
         pair_copy(g).start()
         kept[g, :HEAD_DIM] = key_part[:, :tokens]
         kept[g, HEAD_DIM:] = value_part[:, :tokens]
-        count(2 * g, key_part[:, :tokens], value_part[:, :tokens])
-        count(2 * g + 1, key_part[:, tokens:], value_part[:, tokens:])
 
     def send_home(g):
         pair_copy(g).wait_recv()
@@ -262,47 +255,41 @@
         part_copy(2 * g).start()
 
     kv_copy(1).wait_recv()
-    key_part, value_part = compute(0, True)
-    part_out[1, :HEAD_DIM] = key_part[:, tokens:].astype(BF16)
-    part_out[1, HEAD_DIM:] = value_part[:, tokens:].astype(BF16)
-    part_copy(1).start()
-    own_acc[:HEAD_DIM] = key_part[:, :tokens]
-    own_acc[HEAD_DIM:] = value_part[:, :tokens]
-    count(0, key_part[:, :tokens], value_part[:, :tokens])
-    count(1, key_part[:, tokens:], value_part[:, tokens:])
-    if groups <= 4:
-        for i, g in enumerate(order):
-            if i == 0:
-                pass_on(g)
-            if i + 1 < len(order):
-                pass_on(order[i + 1])
-            turn(g)
-            if i > 0:
-                send_home(order[i - 1])
+    query_side(0, True)
+    if groups == 4:
+        pass_on(1)
+        pass_on(3)
+        turn(1)
+        pass_on(2)
+        turn(3)
+        give(1)
+        turn(2)
+        send_home(1)
     else:
 
         def whole_turn(g, carry):
             pass_on(g)
             turn(g)
-            send_home(g)
             return carry
 
         lax.fori_loop(1, groups, whole_turn, 0)
 
     bias_own[...] = jnp.zeros((BIAS_ROWS, HEAD_DIM), F32)
+    key_bias = jnp.zeros((tokens, HEAD_DIM), F32)
+    value_bias = jnp.zeros((tokens, HEAD_DIM), F32)
     for g in range(GROUP):
-        full = unrotate(dq_acc[g * tokens : (g + 1) * tokens] * SCALE)
-        dq_ref[:, g * HEAD_DIM : (g + 1) * HEAD_DIM] = full.astype(BF16)
+        here = slice(g * tokens, (g + 1) * tokens)
+        cols = slice(g * HEAD_DIM, (g + 1) * HEAD_DIM)
+        full = unrotate(dq_acc[here, :HEAD_DIM] * SCALE)
+        dq_ref[:, cols] = full.astype(BF16)
         bias_own[g : g + 1] = jnp.sum(full, axis=0, keepdims=True)
-    stores[0].start()
-
-    if groups <= 4:
-        send_home(order[-1])
-    sums_t = jnp.transpose(sums[...])
-    key_sums = sums_t[:inners]
-    key_sums = key_sums * start_cos + pltpu.roll(key_sums, half, 1) * start_sin
-    bias_own[GROUP : GROUP + 1] = jnp.sum(key_sums, axis=0, keepdims=True) * SCALE
-    bias_own[GROUP + 1 : GROUP + 2] = jnp.sum(sums_t[half : half + inners], axis=0, keepdims=True)
+        query = q_ref[:, cols].astype(F32)
+        turn_cos, turn_sin = both(dq_acc[here, HEAD_DIM:])
+        key_bias = key_bias + query * turn_cos + pltpu.roll(query, half, 1) * turn_sin
+        weight = jnp.sum(prob_sums[here], axis=1, keepdims=True)
+        value_bias = value_bias + weight * go_ref[:, cols].astype(F32)
+    bias_own[GROUP : GROUP + 1] = jnp.sum(key_bias, axis=0, keepdims=True) * SCALE
+    bias_own[GROUP + 1 : GROUP + 2] = jnp.sum(value_bias, axis=0, keepdims=True)
 
     def bias_copy(step, slot):
         return pltpu.make_async_remote_copy(
@@ -324,18 +311,43 @@
             device_id_type=MESH,
         )
 
+    def bias_along():
+        for step in range(1, inners):
+            bias_copy(step, partner(me, step, inners)).wait_recv()
+        summed = bias_in[0]
+        for slot in range(1, inners):
+            summed = summed + bias_in[slot]
+        plane_own[...] = summed
+        for step in range(1, outers):
+            plane_copy(step, plane).start()
+        plane_in[plane] = summed
+
     for step in range(1, inners):
         bias_copy(step, me).start()
+    stores[0].start()
     bias_in[me] = bias_own[...]
-    for step in range(1, inners):
-        bias_copy(step, partner(me, step, inners)).wait_recv()
-    summed = bias_in[0]
-    for slot in range(1, inners):
-        summed = summed + bias_in[slot]
-    plane_own[...] = summed
-    for step in range(1, outers):
-        plane_copy(step, plane).start()
-    plane_in[plane] = summed
+    if groups == 4:
+        give(3)
+        give(2)
+        send_home(3)
+        bias_along()
+    else:
+
+        def whole_give(g, carry):
+            give(g)
+            send_home(g)
+            return carry
+
+        lax.fori_loop(1, groups, whole_give, 0)
+        bias_along()
+    key_part, value_part = key_side(0)
+    part_out[1, :HEAD_DIM] = key_part[:, tokens:].astype(BF16)
+    part_out[1, HEAD_DIM:] = value_part[:, tokens:].astype(BF16)
+    part_copy(1).start()
+    if groups == 4:
+        send_home(2)
+    own_acc[:HEAD_DIM] = key_part[:, :tokens]
+    own_acc[HEAD_DIM:] = value_part[:, :tokens]
 
     total = own_acc[...]
     for step in direct:
@@ -435,16 +447,16 @@
             pltpu.VMEM((rows, 2 * HEAD_DIM), BF16),
             pltpu.VMEM((HEAD_DIM, rows), BF16),
             pltpu.VMEM((HEAD_DIM, rows), BF16),
-            pltpu.VMEM((rows, 2 * tokens), BF16),
-            pltpu.VMEM((rows, 2 * tokens), BF16),
-            pltpu.VMEM((rows, HEAD_DIM), F32),
+            pltpu.VMEM((inners // 2, rows, 2 * tokens), BF16),
+            pltpu.VMEM((inners // 2, rows, 2 * tokens), BF16),
+            pltpu.VMEM((rows, 2 * HEAD_DIM), F32),
             pltpu.VMEM((2 * HEAD_DIM, tokens), F32),
             pltpu.VMEM((inners // 2, 2 * HEAD_DIM, tokens), F32),
             pltpu.VMEM((inners // 2, 2 * HEAD_DIM, tokens), BF16),
             pltpu.VMEM((inners // 2, 2 * HEAD_DIM, tokens), BF16),
             pltpu.VMEM((inners, 2 * HEAD_DIM, tokens), BF16),
             pltpu.VMEM((inners, 2 * HEAD_DIM, tokens), BF16),
-            pltpu.VMEM((HEAD_DIM, HEAD_DIM), F32),
+            pltpu.VMEM((rows, HEAD_DIM), F32),
             pltpu.VMEM((inners, HEAD_DIM), F32),
             pltpu.VMEM((BIAS_ROWS, HEAD_DIM), F32),
             pltpu.VMEM((inners, BIAS_ROWS, HEAD_DIM), F32),

time: 27.3 us -> 26.3 us (0.963)
  Pallas kernels: 26.5 us -> 25.5 us
    pallas_call x1, Pallas kernels: 24.8 us -> 23.8 us  [local(): pl.pallas_call(functools.partial(kernel, inners, outers), out_shape=shape...]
where the time goes in v6:
time: 26.3 us; the launch traced here: 26.1 us
  Pallas kernels  25.5 us (97%)
  between operations  0.64 us (2%)
    pallas_call x1, Pallas kernels, local(): pl.pallas_call(functools.partial(kernel, inners, outers), out_shape=shape...  23.8 us
    pallas_call x1, Pallas kernels, local(): pl.pallas_call(write, out_shape=shapes, in_specs=[hbm] * 4, out_specs=(hb...  1.71 us

profile of v6, /device:TPU:0, one launch (start us, length us, event | category | flops | bytes accessed | tf_op | source)
XLA Modules:
  0.0 26.1 jit_solution(9337006532366974012)
XLA Ops:
  0.6 23.8 %attention_backward.1 = (bf16[128,896]{1,0:T(8,128)(2,1)}, bf16[128,128]{1,0:T(8,128)(2,1)}, bf16[128,128]{1,0:T(8,128)(2,1)}, f32[36,128]{1,0:T(8,128)}) custom-call(bf16[128,128]{1,0:T(8,128)(2,1)} %bitcast.13, bf16[128,128]{1,0:T(8,128)(2,1)} %bitcast.14, s32[1,128]{1,0:T(1,128)} %seg_hbm.1, bf16[128,896]{1,0:T(8,128)(2,1)} %bitcast.10, ...), custom_call_target="tpu_custom_call" | custom-call | tf_op jit(solution)/shard_map/attention_backward/pallas_call | solution.py:424
  24.4 1.7 %write_results.1 = (bf16[128,896]{1,0:T(8,128)(2,1)}, bf16[128,128]{1,0:T(8,128)(2,1)}, bf16[128,128]{1,0:T(8,128)(2,1)}, f32[36,128]{1,0:T(8,128)}) custom-call(bf16[128,896]{1,0:T(8,128)(2,1)} %get-tuple-element.12.refs_0_, bf16[128,128]{1,0:T(8,128)(2,1)} %get-tuple-element.13.refs_1_, bf16[128,128]{1,0:T(8,128)(2,1)} %get-tuple-element.14.refs_2_, ...), custom_call_target="tpu_custom_call" | custom-call | tf_op jit(solution)/shard_map/write_results/pallas_call | solution.py:478

commit v7 on v6

--- a/solution.py
+++ b/solution.py
@@ -50,7 +50,7 @@
     dq_hbm, dk_hbm, dv_hbm, bias_hbm,
     k_ref, v_ref, seg_ref, q_ref, go_ref, ao_ref, norm_ref, base_ref, starts_ref, load_sem,
     dq_ref, dk_ref, dv_ref, bias_ref, store_sem,
-    kv, q_aug, go_aug, q_t, go_t, probs, grads, dq_acc, own_acc, kept, pair_out, pair_in,
+    kv, q_aug, go_aug, q_t, go_t, probs, grads, scores, pulls, keys, dq_acc, own_acc, kept, pair_out, pair_in,
     part_out, part_in,
     prob_sums, angles, bias_own, bias_in, plane_own, plane_in,
     kv_send, kv_recv, pair_send, pair_recv, part_send, part_recv, bias_send, bias_recv, plane_send, plane_recv,
@@ -207,27 +207,30 @@
     chunk = rows if tokens <= 128 else 256
     starts = list(range(0, rows, chunk))
 
+    tile = 32
+
     def query_side(g, first):
         block = jnp.concatenate([kv[2 * g], kv[2 * g + 1]], axis=1)
         values_t = jnp.concatenate([block[:HEAD_DIM], block[2 * HEAD_DIM :]], axis=0)
         keys_t = block[HEAD_DIM:]
-        turns = jnp.concatenate([waves(2 * g), waves(2 * g + 1)], axis=0)
-        keys = jnp.concatenate([jnp.transpose(block[HEAD_DIM : 2 * HEAD_DIM]), turns], axis=1)
         for start in starts:
             here = slice(start, min(start + chunk, rows))
-            chances = jnp.exp(dot(q_aug[here], keys_t) * SCALE)
+            scores[here] = dot(q_aug[here], keys_t)
+            pulls[here] = dot(go_aug[here], values_t)
+        keys[g, :, :HEAD_DIM] = jnp.transpose(block[HEAD_DIM : 2 * HEAD_DIM])
+        keys[g, :tokens, HEAD_DIM:] = waves(2 * g)
+        keys[g, tokens:, HEAD_DIM:] = waves(2 * g + 1)
+        for start in range(0, rows, tile):
+            here = slice(start, start + tile)
+            chances = jnp.exp(scores[here] * SCALE)
             probs[g, here] = chances.astype(BF16)
-            low_grads = (chances * dot(go_aug[here], values_t)).astype(BF16)
-            grads[g, here] = low_grads
-            part = dot(low_grads, keys)
+            grads[g, here] = (chances * pulls[here]).astype(BF16)
             chance_part = chances[:, :HEAD_DIM]
             for col in range(HEAD_DIM, 2 * tokens, HEAD_DIM):
                 chance_part = chance_part + chances[:, col : col + HEAD_DIM]
             if first:
-                dq_acc[here] = part
                 prob_sums[here] = chance_part
             else:
-                dq_acc[here] += part
                 prob_sums[here] += chance_part
 
     def key_side(g):
@@ -274,6 +277,11 @@
 
         lax.fori_loop(1, groups, whole_turn, 0)
 
+    every_key = jnp.concatenate([keys[g] for g in range(groups)], axis=0)
+    for start in starts:
+        here = slice(start, min(start + chunk, rows))
+        every_grad = jnp.concatenate([grads[g, here] for g in range(groups)], axis=1)
+        dq_acc[here] = dot(every_grad, every_key)
     bias_own[...] = jnp.zeros((BIAS_ROWS, HEAD_DIM), F32)
     key_bias = jnp.zeros((tokens, HEAD_DIM), F32)
     value_bias = jnp.zeros((tokens, HEAD_DIM), F32)
@@ -449,6 +457,9 @@
             pltpu.VMEM((HEAD_DIM, rows), BF16),
             pltpu.VMEM((inners // 2, rows, 2 * tokens), BF16),
             pltpu.VMEM((inners // 2, rows, 2 * tokens), BF16),
+            pltpu.VMEM((rows, 2 * tokens), F32),
+            pltpu.VMEM((rows, 2 * tokens), F32),
+            pltpu.VMEM((inners // 2, 2 * tokens, 2 * HEAD_DIM), BF16),
             pltpu.VMEM((rows, 2 * HEAD_DIM), F32),
             pltpu.VMEM((2 * HEAD_DIM, tokens), F32),
             pltpu.VMEM((inners // 2, 2 * HEAD_DIM, tokens), F32),

time: 26.3 us -> 26 us (0.989)
  Pallas kernels: 25.5 us -> 25.2 us
    pallas_call x1, Pallas kernels: 23.8 us -> 23.5 us  [local(): pl.pallas_call(functools.partial(kernel, inners, outers), out_shape=shape...]
where the time goes in v7:
time: 26 us; the launch traced here: 25.8 us
  Pallas kernels  25.2 us (97%)
  between operations  0.64 us (2%)
    pallas_call x1, Pallas kernels, local(): pl.pallas_call(functools.partial(kernel, inners, outers), out_shape=shape...  23.5 us
    pallas_call x1, Pallas kernels, local(): pl.pallas_call(write, out_shape=shapes, in_specs=[hbm] * 4, out_specs=(hb...  1.71 us

profile of v7, /device:TPU:0, one launch (start us, length us, event | category | flops | bytes accessed | tf_op | source)
XLA Modules:
  0.0 25.8 jit_solution(7985971280648931829)
XLA Ops:
  0.6 23.5 %attention_backward.1 = (bf16[128,896]{1,0:T(8,128)(2,1)}, bf16[128,128]{1,0:T(8,128)(2,1)}, bf16[128,128]{1,0:T(8,128)(2,1)}, f32[36,128]{1,0:T(8,128)}) custom-call(bf16[128,128]{1,0:T(8,128)(2,1)} %bitcast.13, bf16[128,128]{1,0:T(8,128)(2,1)} %bitcast.14, s32[1,128]{1,0:T(1,128)} %seg_hbm.1, bf16[128,896]{1,0:T(8,128)(2,1)} %bitcast.10, ...), custom_call_target="tpu_custom_call" | custom-call | tf_op jit(solution)/shard_map/attention_backward/pallas_call | solution.py:432
  24.1 1.7 %write_results.1 = (bf16[128,896]{1,0:T(8,128)(2,1)}, bf16[128,128]{1,0:T(8,128)(2,1)}, bf16[128,128]{1,0:T(8,128)(2,1)}, f32[36,128]{1,0:T(8,128)}) custom-call(bf16[128,896]{1,0:T(8,128)(2,1)} %get-tuple-element.12.refs_0_, bf16[128,128]{1,0:T(8,128)(2,1)} %get-tuple-element.13.refs_1_, bf16[128,128]{1,0:T(8,128)(2,1)} %get-tuple-element.14.refs_2_, ...), custom_call_target="tpu_custom_call" | custom-call | tf_op jit(solution)/shard_map/write_results/pallas_call | solution.py:489

commit v8 on v7

--- a/solution.py
+++ b/solution.py
@@ -102,8 +102,6 @@
     for slot in range(inners):
         kv[slot, 2 * HEAD_DIM + EXTRA :] = jnp.zeros((HEAD_DIM - EXTRA, tokens), BF16)
 
-    pl.semaphore_wait(barrier, inners + outers - 2)
-
     sent = 2 * HEAD_DIM + EXTRA
 
     def kv_copy(step):
@@ -148,9 +146,6 @@
 
     groups = inners // 2
     direct = [1] + [2 * g for g in range(1, groups)]
-    for step in direct:
-        kv_copy(step).start()
-
     for load in loads[3:]:
         load.wait()
     row8 = lax.broadcasted_iota(jnp.int32, (8, tokens), 0)
@@ -165,8 +160,6 @@
         grad = go_ref[:, cols]
         q_aug[here, :HEAD_DIM] = query
         go_aug[here, :HEAD_DIM] = grad
-        q_t[:, here] = jnp.transpose(query)
-        go_t[:, here] = jnp.transpose(grad)
         high, middle, low = pieces(norm_ref[g] * -ROOT)
         top = jnp.where(row8 == 0, high, masks)
         top = jnp.where(row8 == 1, middle, top)
@@ -236,6 +229,13 @@
     def key_side(g):
         return dot(q_t[...], grads[g]), dot(go_t[...], probs[g])
 
+    def turn_over():
+        for g in range(GROUP):
+            here = slice(g * tokens, (g + 1) * tokens)
+            cols = slice(g * HEAD_DIM, (g + 1) * HEAD_DIM)
+            q_t[:, here] = jnp.transpose(q_ref[:, cols])
+            go_t[:, here] = jnp.transpose(go_ref[:, cols])
+
     def pass_on(g):
         kv_copy(2 * g).wait_recv()
         forward(2 * g).start()
@@ -257,11 +257,16 @@
         part_out[2 * g] = (kept[g] + pair_in[g].astype(F32)).astype(BF16)
         part_copy(2 * g).start()
 
+    pl.semaphore_wait(barrier, inners + outers - 2)
+    for step in direct:
+        kv_copy(step).start()
+
     kv_copy(1).wait_recv()
     query_side(0, True)
     if groups == 4:
         pass_on(1)
         pass_on(3)
+        turn_over()
         turn(1)
         pass_on(2)
         turn(3)
@@ -269,6 +274,7 @@
         turn(2)
         send_home(1)
     else:
+        turn_over()
 
         def whole_turn(g, carry):
             pass_on(g)

time: 26 us -> 26 us (level)
  no operation moved by 1% of the time
where the time goes in v8:
time: 26 us; the launch traced here: 25.8 us
  Pallas kernels  25.2 us (97%)
  between operations  0.64 us (2%)
    pallas_call x1, Pallas kernels, local(): pl.pallas_call(functools.partial(kernel, inners, outers), out_shape=shape...  23.5 us
    pallas_call x1, Pallas kernels, local(): pl.pallas_call(write, out_shape=shapes, in_specs=[hbm] * 4, out_specs=(hb...  1.71 us

profile of v8, /device:TPU:0, one launch (start us, length us, event | category | flops | bytes accessed | tf_op | source)
XLA Modules:
  0.0 25.8 jit_solution(17094611040055141152)
XLA Ops:
  0.6 23.5 %attention_backward.1 = (bf16[128,896]{1,0:T(8,128)(2,1)}, bf16[128,128]{1,0:T(8,128)(2,1)}, bf16[128,128]{1,0:T(8,128)(2,1)}, f32[36,128]{1,0:T(8,128)}) custom-call(bf16[128,128]{1,0:T(8,128)(2,1)} %bitcast.13, bf16[128,128]{1,0:T(8,128)(2,1)} %bitcast.14, s32[1,128]{1,0:T(1,128)} %seg_hbm.1, bf16[128,896]{1,0:T(8,128)(2,1)} %bitcast.10, ...), custom_call_target="tpu_custom_call" | custom-call | tf_op jit(solution)/shard_map/attention_backward/pallas_call | solution.py:438
  24.1 1.7 %write_results.1 = (bf16[128,896]{1,0:T(8,128)(2,1)}, bf16[128,128]{1,0:T(8,128)(2,1)}, bf16[128,128]{1,0:T(8,128)(2,1)}, f32[36,128]{1,0:T(8,128)}) custom-call(bf16[128,896]{1,0:T(8,128)(2,1)} %get-tuple-element.12.refs_0_, bf16[128,128]{1,0:T(8,128)(2,1)} %get-tuple-element.13.refs_1_, bf16[128,128]{1,0:T(8,128)(2,1)} %get-tuple-element.14.refs_2_, ...), custom_call_target="tpu_custom_call" | custom-call | tf_op jit(solution)/shard_map/write_results/pallas_call | solution.py:495

commit v9 on v8

--- a/solution.py
+++ b/solution.py
@@ -153,9 +153,14 @@
     masks = jnp.where((row8 == 3) & (seg8 != 1.0), MASKED, 0.0)
     masks = jnp.where((row8 == 4) & (seg8 != 2.0), MASKED, masks)
     lane = lax.broadcasted_iota(jnp.int32, (tokens, HEAD_DIM), 1)
-    for g in range(GROUP):
-        here = slice(g * tokens, (g + 1) * tokens)
-        cols = slice(g * HEAD_DIM, (g + 1) * HEAD_DIM)
+    def head_at(g):
+        return (
+            pl.ds(pl.multiple_of(g * tokens, tokens), tokens),
+            pl.ds(pl.multiple_of(g * HEAD_DIM, HEAD_DIM), HEAD_DIM),
+        )
+
+    def prepare(g, carry):
+        here, cols = head_at(g)
         query = q_ref[:, cols]
         grad = go_ref[:, cols]
         q_aug[here, :HEAD_DIM] = query
@@ -174,6 +179,9 @@
         side = jnp.where(lane == 1, d_middle, side)
         side = jnp.where(lane == 2, d_low, side)
         go_aug[here, HEAD_DIM:] = side.astype(BF16)
+        return carry
+
+    lax.fori_loop(0, GROUP, prepare, 0)
 
     half = HEAD_DIM // 2
     for slot in range(inners):
@@ -202,7 +210,7 @@
 
     tile = 32
 
-    def query_side(g, first):
+    def query_side(g):
         block = jnp.concatenate([kv[2 * g], kv[2 * g + 1]], axis=1)
         values_t = jnp.concatenate([block[:HEAD_DIM], block[2 * HEAD_DIM :]], axis=0)
         keys_t = block[HEAD_DIM:]
@@ -213,36 +221,33 @@
         keys[g, :, :HEAD_DIM] = jnp.transpose(block[HEAD_DIM : 2 * HEAD_DIM])
         keys[g, :tokens, HEAD_DIM:] = waves(2 * g)
         keys[g, tokens:, HEAD_DIM:] = waves(2 * g + 1)
-        for start in range(0, rows, tile):
-            here = slice(start, start + tile)
-            chances = jnp.exp(scores[here] * SCALE)
-            probs[g, here] = chances.astype(BF16)
-            grads[g, here] = (chances * pulls[here]).astype(BF16)
-            chance_part = chances[:, :HEAD_DIM]
-            for col in range(HEAD_DIM, 2 * tokens, HEAD_DIM):
-                chance_part = chance_part + chances[:, col : col + HEAD_DIM]
-            if first:
-                prob_sums[here] = chance_part
-            else:
+
+        def one_stretch(i, carry):
+            for start in range(0, HEAD_DIM, tile):
+                here = pl.ds(pl.multiple_of(i * HEAD_DIM + start, tile), tile)
+                chances = jnp.exp(scores[here] * SCALE)
+                probs[g, here] = chances.astype(BF16)
+                grads[g, here] = (chances * pulls[here]).astype(BF16)
+                chance_part = chances[:, :HEAD_DIM]
+                for col in range(HEAD_DIM, 2 * tokens, HEAD_DIM):
+                    chance_part = chance_part + chances[:, col : col + HEAD_DIM]
                 prob_sums[here] += chance_part
+            return carry
+
+        lax.fori_loop(0, rows // HEAD_DIM, one_stretch, 0)
 
     def key_side(g):
         return dot(q_t[...], grads[g]), dot(go_t[...], probs[g])
 
-    def turn_over():
-        for g in range(GROUP):
-            here = slice(g * tokens, (g + 1) * tokens)
-            cols = slice(g * HEAD_DIM, (g + 1) * HEAD_DIM)
-            q_t[:, here] = jnp.transpose(q_ref[:, cols])
-            go_t[:, here] = jnp.transpose(go_ref[:, cols])
+    def turn_over(g, carry):
+        here, cols = head_at(g)
+        q_t[:, here] = jnp.transpose(q_ref[:, cols])
+        go_t[:, here] = jnp.transpose(go_ref[:, cols])
+        return carry
 
     def pass_on(g):
         kv_copy(2 * g).wait_recv()
         forward(2 * g).start()
-
-    def turn(g):
-        forward(2 * g).wait_recv()
-        query_side(g, False)
 
     def give(g):
         key_part, value_part = key_side(g)
@@ -261,27 +266,31 @@
     for step in direct:
         kv_copy(step).start()
 
-    kv_copy(1).wait_recv()
-    query_side(0, True)
-    if groups == 4:
-        pass_on(1)
-        pass_on(3)
-        turn_over()
-        turn(1)
-        pass_on(2)
-        turn(3)
-        give(1)
-        turn(2)
-        send_home(1)
-    else:
-        turn_over()
-
-        def whole_turn(g, carry):
-            pass_on(g)
-            turn(g)
-            return carry
-
-        lax.fori_loop(1, groups, whole_turn, 0)
+    prob_sums[...] = jnp.zeros((rows, HEAD_DIM), F32)
+    lax.fori_loop(0, GROUP, turn_over, 0)
+
+    def one_group(g, carry):
+        @pl.when(g == 0)
+        def _():
+            kv_copy(1).wait_recv()
+
+        @pl.when(g > 0)
+        def _():
+            forward(2 * g).wait_recv()
+
+        query_side(g)
+
+        @pl.when(g == 0)
+        def _():
+            pass_on(1)
+
+        @pl.when(g + 2 < groups)
+        def _():
+            pass_on(g + 2)
+
+        return carry
+
+    lax.fori_loop(0, groups, one_group, 0)
 
     every_key = jnp.concatenate([keys[g] for g in range(groups)], axis=0)
     for start in starts:
@@ -289,19 +298,21 @@
         every_grad = jnp.concatenate([grads[g, here] for g in range(groups)], axis=1)
         dq_acc[here] = dot(every_grad, every_key)
     bias_own[...] = jnp.zeros((BIAS_ROWS, HEAD_DIM), F32)
-    key_bias = jnp.zeros((tokens, HEAD_DIM), F32)
-    value_bias = jnp.zeros((tokens, HEAD_DIM), F32)
-    for g in range(GROUP):
-        here = slice(g * tokens, (g + 1) * tokens)
-        cols = slice(g * HEAD_DIM, (g + 1) * HEAD_DIM)
+    def finish(g, carry):
+        key_bias, value_bias = carry
+        here, cols = head_at(g)
         full = unrotate(dq_acc[here, :HEAD_DIM] * SCALE)
         dq_ref[:, cols] = full.astype(BF16)
-        bias_own[g : g + 1] = jnp.sum(full, axis=0, keepdims=True)
+        bias_own[pl.ds(g, 1)] = jnp.sum(full, axis=0, keepdims=True)
         query = q_ref[:, cols].astype(F32)
         turn_cos, turn_sin = both(dq_acc[here, HEAD_DIM:])
         key_bias = key_bias + query * turn_cos + pltpu.roll(query, half, 1) * turn_sin
         weight = jnp.sum(prob_sums[here], axis=1, keepdims=True)
         value_bias = value_bias + weight * go_ref[:, cols].astype(F32)
+        return key_bias, value_bias
+
+    nothing = jnp.zeros((tokens, HEAD_DIM), F32)
+    key_bias, value_bias = lax.fori_loop(0, GROUP, finish, (nothing, nothing))
     bias_own[GROUP : GROUP + 1] = jnp.sum(key_bias, axis=0, keepdims=True) * SCALE
     bias_own[GROUP + 1 : GROUP + 2] = jnp.sum(value_bias, axis=0, keepdims=True)
 
@@ -340,26 +351,23 @@
         bias_copy(step, me).start()
     stores[0].start()
     bias_in[me] = bias_own[...]
-    if groups == 4:
-        give(3)
-        give(2)
-        send_home(3)
-        bias_along()
-    else:
-
-        def whole_give(g, carry):
-            give(g)
-            send_home(g)
-            return carry
-
-        lax.fori_loop(1, groups, whole_give, 0)
-        bias_along()
+
+    def one_gift(g, carry):
+        give(g)
+
+        @pl.when(g > 1)
+        def _():
+            send_home(g - 1)
+
+        return carry
+
+    lax.fori_loop(1, groups, one_gift, 0)
+    bias_along()
     key_part, value_part = key_side(0)
     part_out[1, :HEAD_DIM] = key_part[:, tokens:].astype(BF16)
     part_out[1, HEAD_DIM:] = value_part[:, tokens:].astype(BF16)
     part_copy(1).start()
-    if groups == 4:
-        send_home(2)
+    send_home(groups - 1)
     own_acc[:HEAD_DIM] = key_part[:, :tokens]
     own_acc[HEAD_DIM:] = value_part[:, :tokens]
 

time: 26 us -> 25.9 us (level)
  no operation moved by 1% of the time
where the time goes in v9:
time: 25.9 us; the launch traced here: 25.8 us
  Pallas kernels  25.1 us (97%)
  between operations  0.64 us (2%)
    pallas_call x1, Pallas kernels, local(): pl.pallas_call(functools.partial(kernel, inners, outers), out_shape=shape...  23.4 us
    pallas_call x1, Pallas kernels, local(): pl.pallas_call(write, out_shape=shapes, in_specs=[hbm] * 4, out_specs=(hb...  1.71 us

profile of v9, /device:TPU:0, one launch (start us, length us, event | category | flops | bytes accessed | tf_op | source)
XLA Modules:
  0.0 25.8 jit_solution(4056996715910324674)
XLA Ops:
  0.6 23.4 %attention_backward.1 = (bf16[128,896]{1,0:T(8,128)(2,1)}, bf16[128,128]{1,0:T(8,128)(2,1)}, bf16[128,128]{1,0:T(8,128)(2,1)}, f32[36,128]{1,0:T(8,128)}) custom-call(bf16[128,128]{1,0:T(8,128)(2,1)} %bitcast.13, bf16[128,128]{1,0:T(8,128)(2,1)} %bitcast.14, s32[1,128]{1,0:T(1,128)} %seg_hbm.1, bf16[128,896]{1,0:T(8,128)(2,1)} %bitcast.10, ...), custom_call_target="tpu_custom_call" | custom-call | tf_op jit(solution)/shard_map/attention_backward/pallas_call | solution.py:446
  24.0 1.7 %write_results.1 = (bf16[128,896]{1,0:T(8,128)(2,1)}, bf16[128,128]{1,0:T(8,128)(2,1)}, bf16[128,128]{1,0:T(8,128)(2,1)}, f32[36,128]{1,0:T(8,128)}) custom-call(bf16[128,896]{1,0:T(8,128)(2,1)} %get-tuple-element.12.refs_0_, bf16[128,128]{1,0:T(8,128)(2,1)} %get-tuple-element.13.refs_1_, bf16[128,128]{1,0:T(8,128)(2,1)} %get-tuple-element.14.refs_2_, ...), custom_call_target="tpu_custom_call" | custom-call | tf_op jit(solution)/shard_map/write_results/pallas_call | solution.py:503
